TPU v7x, 512 devices: a whole 4x4x16 slice. The times are simulated.
512 devices in a mesh: dp: 16 (over y, x), shard: 32 (over z, core).
Axes of the slice: x: 4, y: 4, z: 16, core: 2. Of those that a mesh axis runs over, the one named last changes fastest.
Arguments:
- grad_parts: bfloat16 [16, 384, 256, 256], P('dp', 'shard'), may hold values from -4.5 to 4.5
- owner_list: int32 [384, 1], P('shard'), may hold values from 0 to 15; in each aligned block of 12 rows (0 to 11, 12 to 23, ...) at most 2 rows name the same one
- left_stats: float32 [16, 32, 2, 256, 256], P('dp', 'shard'), may hold values from -9 to 2560, as said below
- right_stats: float32 [16, 32, 2, 256, 256], P('dp', 'shard'), may hold values from -9 to 2560, as said below
Outputs:
- update: bfloat16 [384, 256, 256], P('shard')
- left_new: float32 [16, 32, 2, 256, 256], P('dp', 'shard')
- right_new: float32 [16, 32, 2, 256, 256], P('dp', 'shard')
Inputs may be any that keep to these rules, and one draw needn't show every extreme that they name: `owner_list`: within each column (aligned blocks of 12 consecutive blocks) no owner index is named more than 2 times. `left_stats`: each matrix is symmetric positive definite. `right_stats`: each matrix is symmetric positive definite.
All inputs are finite; a program needn't handle non-finite values.
Results may differ from a plain program's by a relative error of at most 0.001.
Values may be sent and summed in bfloat16 or wider, within the bound.
A program may use at most 64 MiB of HBM per device.

v0:
```python
import jax
import jax.numpy as jnp
from jax import lax
from jax.sharding import PartitionSpec as P

ITERS = 4


DECAY_RATE = 0.9
ROOT_ORDER = 4.0
RIDGE_SCALE = 0.01


def batched(form, first, second):
    return jnp.einsum(
        form, first, second, precision=lax.Precision.HIGHEST, preferred_element_type=jnp.float32
    )


def slot_ranks(owner_column):
    block_count = owner_column.shape[0]
    same_owner = owner_column[:, None] == owner_column[None, :]
    earlier = jnp.arange(block_count)[:, None] > jnp.arange(block_count)[None, :]
    return jnp.sum((same_owner & earlier).astype(jnp.int32), axis=1)


def inverse_root(statistic):
    block_width = statistic.shape[1]
    identity = jnp.eye(block_width, dtype=jnp.float32)[None]
    traces = jnp.trace(statistic, axis1=1, axis2=2)
    shifted = statistic + (RIDGE_SCALE * traces / block_width)[:, None, None] * identity
    norm_scale = (ROOT_ORDER + 1.0) / (
        2.0 * jnp.sqrt(jnp.sum(shifted * shifted, axis=(1, 2)) + 1e-06)
    )
    root_mat = (norm_scale ** (1.0 / ROOT_ORDER))[:, None, None] * identity
    power_mat = norm_scale[:, None, None] * shifted
    for iteration in range(ITERS):
        factor = ((ROOT_ORDER + 1.0) * identity - power_mat) / ROOT_ORDER
        root_mat = batched("kij,kjl->kil", root_mat, factor)
        square = batched("kij,kjl->kil", factor, factor)
        power_mat = batched("kij,kjl->kil", batched("kij,kjl->kil", square, square), power_mat)
    return root_mat


def local(grad_parts, owner_list, left_stats, right_stats):
    partials = grad_parts[0].astype(jnp.float32)
    block_count = partials.shape[0]
    capacity = left_stats.shape[2]
    owners = owner_list[:, 0]
    slot_rank = slot_ranks(owners)
    own_index = lax.axis_index("dp")
    summed = lax.psum(partials, "dp")
    matches = (owners[None, :] == own_index) & (slot_rank[None, :] == jnp.arange(capacity)[:, None])
    in_use = jnp.any(matches, axis=1).astype(jnp.float32)
    picked = jnp.sum(jnp.where(matches, jnp.arange(block_count)[None, :], 0), axis=1)
    grads = jnp.take(summed, picked, axis=0) * in_use[:, None, None]
    left_next = DECAY_RATE * left_stats[0, 0] + (1.0 - DECAY_RATE) * batched(
        "kij,klj->kil", grads, grads
    )
    right_next = DECAY_RATE * right_stats[0, 0] + (1.0 - DECAY_RATE) * batched(
        "kji,kjl->kil", grads, grads
    )
    root_left = inverse_root(left_next)
    root_right = inverse_root(right_next)
    directions = batched("kij,kjl->kil", batched("kij,kjl->kil", root_left, grads), root_right)
    grad_mean = jnp.mean(grads * grads, axis=(1, 2))
    dir_mean = jnp.mean(directions * directions, axis=(1, 2))
    graft_ratio = jnp.sqrt(grad_mean) / jnp.sqrt(dir_mean + 1e-06)
    scaled = (directions * graft_ratio[:, None, None]).astype(jnp.bfloat16)
    all_slots = lax.all_gather(scaled, "dp", axis=0, tiled=True)
    update = jnp.take(all_slots, owners * capacity + slot_rank, axis=0)
    return (update, left_next[None, None], right_next[None, None])


def solution(mesh):
    return jax.shard_map(
        local,
        mesh=mesh,
        in_specs=(
            P("dp", "shard", None, None),
            P("shard", None),
            P("dp", "shard", None, None, None),
            P("dp", "shard", None, None, None),
        ),
        out_specs=(
            P("shard", None, None),
            P("dp", "shard", None, None, None),
            P("dp", "shard", None, None, None),
        ),
        check_vma=False,
    )
```

profile of v0, /device:TPU:1, one launch (start us, length us, event | category | flops | bytes accessed | tf_op | source)
XLA Modules:
  0.0 246.8 jit_solution(15324152321134371221)
XLA Ops:
  7.2 0.0 all-reduce.2.cloned.1.call-start
  7.2 3.4 %bitcast_convert_fusion = f32[12,256,256]{2,1,0:T(8,128)} fusion(bf16[1,12,256,256]{3,2,1,0:T(8,128)(2,1)} %param.4), kind=kLoop, calls=%fused_computation.2 | loop fusion | flops 786432 | bytes 4718592 | tf_op jit(solution)/shard_map/convert_element_type | solution.py:46
  10.6 0.0 all-reduce.2.cloned.1.call-update
  10.7 0.0 all-gather.2.cloned.1.call-start
  10.7 0.6 copy-done.4
  11.3 0.2 convert_reduce_fusion
  11.5 0.1 fusion.79
  11.6 0.1 select_reduce_fusion.2
  11.9 130.9 %all-reduce.2.cloned.1.call-done = f32[12,256,256]{2,1,0:T(8,128)} async-done(((f32[12,256,256]{2,1,0:T(8,128)}), f32[12,256,256]{2,1,0:T(8,128)}) %all-reduce.2.cloned.1.call-update) | async-done | bytes 3145744 | tf_op jit(solution)/shard_map/psum | solution.py:52
  142.7 2.5 gather_fusion
  145.2 0.2 multiply_reduce_fusion.1
  145.4 0.9 fusion.3
  146.3 0.0 copy-start
  146.3 1.2 select_reduce_fusion
  147.6 0.3 multiply_reduce_fusion.2
  147.9 0.9 fusion.21
  148.8 0.6 fusion.101
  149.5 0.8 fusion.8
  150.3 0.7 fusion.16
  151.0 0.6 fusion.102
  151.7 0.7 fusion.103
  152.3 0.7 fusion.18
  153.0 0.6 fusion.104
  153.7 0.7 fusion
  154.4 0.8 fusion.4
  155.2 0.7 fusion.17
  155.9 0.7 fusion.19
  156.6 0.9 fusion.20
  157.5 0.8 fusion.96
  158.4 0.8 fusion.10
  159.1 0.7 fusion.12
  159.9 0.6 fusion.97
  160.5 0.7 fusion.98
  161.2 0.7 fusion.14
  161.9 0.7 fusion.99
  162.6 0.7 fusion.2
  163.3 0.8 fusion.6
  164.1 0.7 fusion.13
  164.8 0.7 fusion.15
  165.5 0.7 fusion.100
  166.1 0.8 fusion.22
  166.9 0.7 fusion.105
  167.6 0.8 multiply_reduce_fusion
  168.3 0.8 multiply_convert_fusion
  169.1 0.0 all-gather.2.cloned.1.call-update
  169.2 66.6 %all-gather.2.cloned.1.call-done = bf16[32,256,256]{2,1,0:T(8,128)(2,1)} async-done(((bf16[2,256,256]{2,1,0:T(8,128)(2,1)}), bf16[32,256,256]{2,1,0:T(8,128)(2,1)}) %all-gather.2.cloned.1.call-update) | async-done | bytes 4194320 | tf_op jit(solution)/shard_map/all_gather | solution.py:70
  235.8 2.8 %gather_fusion.1 = bf16[12,256,256]{2,1,0:T(8,128)(2,1)S(1)} fusion(bf16[32,256,256]{2,1,0:T(8,128)(2,1)} %all-gather.2.cloned.1.call-done, s32[1024]{0:T(1024)S(1)} %pad_clamp_fusion), kind=kCustom, calls=%fused_computation.1 | custom fusion | bytes 3145776 | tf_op jit(solution)/shard_map/jit(_take)/gather | solution.py:71
  238.6 1.4 broadcast_select_fusion
  (22 shorter events, 0.2 us)
Async XLA Ops:
  7.2 135.5 %all-reduce.2.cloned.1.call-start = ((), (), s32[]{:S(2)}) async-start(), calls=%async_computation | async-start | bytes 6291456 | tf_op jit(solution)/shard_map/psum | solution.py:52
  10.6 0.7 copy-start.4
  10.7 134.8 %copy-start.3 = (f32[1,1,2,256,256]{4,3,2,1,0:T(8,128)S(1)}, f32[1,1,2,256,256]{4,3,2,1,0:T(8,128)}, u32[]{:S(2)}) copy-start(f32[1,1,2,256,256]{4,3,2,1,0:T(8,128)} %param.6) | copy-start | bytes 1572868
  10.7 225.1 %all-gather.2.cloned.1.call-start = ((), (), s32[]{:S(2)}) async-start(), calls=%async_computation.1 | async-start | bytes 4456448 | tf_op jit(solution)/shard_map/all_gather | solution.py:70
  11.8 134.4 %copy-start.2 = (f32[1,1,2,256,256]{4,3,2,1,0:T(8,128)S(1)}, f32[1,1,2,256,256]{4,3,2,1,0:T(8,128)}, u32[]{:S(2)}) copy-start(f32[1,1,2,256,256]{4,3,2,1,0:T(8,128)} %param.7) | copy-start | bytes 1572868
  146.3 17.0 %copy-start = (f32[2,256,256]{2,1,0:T(8,128)}, f32[2,256,256]{2,1,0:T(8,128)S(1)}, u32[]{:S(2)}) copy-start(f32[2,256,256]{2,1,0:T(8,128)S(1)} %fusion.3) | copy-start | bytes 1572868
  147.6 6.8 %copy-start.1 = (f32[2,256,256]{2,1,0:T(8,128)}, f32[2,256,256]{2,1,0:T(8,128)S(1)}, u32[]{:S(2)}) copy-start(f32[2,256,256]{2,1,0:T(8,128)S(1)} %get-tuple-element.13) | copy-start | bytes 1572868
Sparse Core Ops, SparseCore 0:
  11.4 131.3 all-reduce.1
  169.3 66.4 all-gather.1
where the time goes:
time: 247 us
  waiting for transfers between devices  197 us (80%)
  matrix products  22.3 us (9%)
  between operations  14.4 us (6%)
  other arithmetic  6.73 us (3%)
  local copies, waits for them, and re-layouts  5.89 us (2%)
    psum x1, waiting for transfers between devices, local(): summed = lax.psum(partials, 'dp')  131 us
    all_gather x1, waiting for transfers between devices, local(): all_slots = lax.all_gather(scaled, 'dp', axis=0, tiled=True)  66.6 us
    dot_general x30, matrix products, batched(): jnp.einsum(form, first, second, precision=lax.Precision.HIGHEST, preferre...  22.3 us
  transfers between devices with their start and end apart: 2, of which 2 were waited for; matrix products, arithmetic and copies ran while one was open for 0% of the time, Pallas kernels for 0%

commit v1 on v0

v1 whole, which is shorter than its diff:
```python
import functools

import jax
import jax.numpy as jnp
from jax import lax
from jax.experimental import pallas as pl
from jax.experimental.pallas import tpu as pltpu
from jax.sharding import PartitionSpec as P

ITERS = 4
DECAY = 0.9
RIDGE = 0.01
ROWS = 16
HALF = 6
BF16, F32 = jnp.bfloat16, jnp.float32
MESH = pl.DeviceIdType.MESH
A, B0, B1, C0, C1, D0, D1 = range(7)


def split(value):
    high = value.astype(BF16)
    return high, (value - high.astype(F32)).astype(BF16)


def product(first, second):
    (ah, al), (bh, bl) = first, second
    return jnp.dot(
        jnp.concatenate([ah, ah, al], axis=1),
        jnp.concatenate([bh, bl, bh], axis=0),
        preferred_element_type=F32,
    )


def total(value):
    return jnp.sum(jnp.sum(value, axis=0, keepdims=True), axis=1, keepdims=True)


def ranks_of(owners):
    ranks = []
    for b, owner in enumerate(owners):
        rank = jnp.int32(0)
        for other in owners[:b]:
            rank = rank + jnp.where(other == owner, 1, 0)
        ranks.append(rank)
    firsts = sum(jnp.where(rank == 0, 1, 0) for rank in ranks)
    places, first, second = [], jnp.int32(0), firsts
    for rank in ranks:
        places.append(jnp.where(rank == 0, first, second))
        first = first + jnp.where(rank == 0, 1, 0)
        second = second + jnp.where(rank == 0, 0, 1)
    return ranks, places


def chosen(tests, values):
    return sum(jnp.where(test, value, 0) for test, value in zip(tests, values))


class Root:
    def __init__(self, statistic, eye):
        width = statistic.shape[0]
        shift = total(jnp.where(eye, statistic, 0.0)) * (RIDGE / width)
        shifted = statistic + jnp.where(eye, shift, 0.0)
        scale = 2.5 / jnp.sqrt(total(shifted * shifted) + 1e-06)
        self.eye = eye
        self.gain = jnp.sqrt(jnp.sqrt(scale))
        self.power = scale * shifted
        self.next_factor()

    def next_factor(self):
        self.factor = split(jnp.where(self.eye, 1.25, 0.0) - 0.25 * self.power)

    def advance(self):
        square = split(product(self.factor, self.factor))
        fourth = split(product(square, square))
        self.power = product(fourth, split(self.power))
        self.next_factor()


def kernel(
    side, own_ref, g_ref, ls_ref, rs_ref, upd_ref, ln_ref, rn_ref,
    parts, acc, picked0, picked1, grad0, grad1, left, right, left_out, right_out,
    ready0, ready1, home0, home1, gather0, gather1,
    owner_at, slot_at, block_at, send, recv, local,
):
    n = side * side
    blocks = own_ref.shape[0]
    me = lax.axis_index("dp")
    row, col = me // side, me % side

    def peer(k):
        return ((row + k // side) % side) * side + (col + k % side) % side

    barrier = pltpu.get_barrier_semaphore()

    @pl.loop(1, n)
    def _(k):
        pl.semaphore_signal(barrier, inc=1, device_id={"dp": peer(k)}, device_id_type=MESH)

    pl.semaphore_wait(barrier, n - 1)

    def copy(stage, k, src, dst):
        return pltpu.make_async_remote_copy(
            src_ref=src, dst_ref=dst, send_sem=send.at[stage, k], recv_sem=recv.at[stage, k],
            device_id={"dp": peer(k)}, device_id_type=MESH,
        )

    def part_copy(k):
        return copy(A, k, g_ref.at[:, peer(k)], parts.at[k])

    def slot_copy(slot, k):
        return copy((B0, B1)[slot], k, (picked0, picked1)[slot].at[k], (grad0, grad1)[slot].at[me])

    def home_copy(slot, k):
        return copy(
            (C0, C1)[slot], k, (ready0, ready1)[slot].at[peer(k)], (home0, home1)[slot].at[me]
        )

    def gather_copy(half, k):
        return copy(
            (D0, D1)[half], k, (gather0, gather1)[half], upd_ref.at[pl.ds(half * HALF, HALF), me]
        )

    @pl.loop(1, n)
    def _(k):
        part_copy(k).start()

    mine = pltpu.make_async_copy(g_ref.at[:, me], parts.at[0], local.at[0])
    mine.start()
    stats = [
        pltpu.make_async_copy(ls_ref, left, local.at[1]),
        pltpu.make_async_copy(rs_ref, right, local.at[2]),
    ]
    for each in stats:
        each.start()

    owners = [own_ref[b] for b in range(blocks)]
    ranks, places = ranks_of(owners)

    @pl.loop(0, n)
    def _(k):
        to = peer(k)
        for slot in range(2):
            tests = [(o == to) & (r == slot) for o, r in zip(owners, ranks)]
            block_at[slot, k] = chosen(tests, range(blocks))

    @pl.loop(0, blocks)
    def _(p):
        tests = [place == p for place in places]
        owner_at[p] = chosen(tests, owners)
        slot_at[p] = chosen(tests, ranks)

    used = [
        chosen([(o == me) & (r == slot) for o, r in zip(owners, ranks)], [1] * blocks) > 0
        for slot in range(2)
    ]

    mine.wait()
    acc[...] = parts[0].astype(F32)

    @pl.loop(1, n)
    def _(k):
        part_copy(k).wait_recv()
        acc[...] += parts[k].astype(F32)

    for slot in range(2):
        grad, picked = (grad0, grad1)[slot], (picked0, picked1)[slot]

        @pl.loop(1, n)
        def _(k):
            picked[k] = acc[block_at[slot, k]]
            slot_copy(slot, k).start()

        grad[me] = acc[block_at[slot, 0]]

    for each in stats:
        each.wait()

    def gather_half(half):
        @pl.loop(1, n)
        def _(k):
            home_copy(half, k).wait_recv()

        for p in range(HALF):
            at = half * HALF + p
            if half == 0:
                gather0[p] = home0[owner_at[at]]
            else:
                gather1[p] = jnp.where(slot_at[at] == 0, home0[owner_at[at]], home1[owner_at[at]])

        @pl.loop(1, n)
        def _(k):
            gather_copy(half, k).start()

    for slot in range(2):
        grad, ready, home = (grad0, grad1)[slot], (ready0, ready1)[slot], (home0, home1)[slot]

        @pl.loop(1, n)
        def _(k):
            slot_copy(slot, k).wait_recv()

        width = left.shape[1]
        value = jnp.where(used[slot], grad[...].reshape(width, width), 0.0)
        eye = lax.broadcasted_iota(jnp.int32, (width, width), 0) == lax.broadcasted_iota(
            jnp.int32, (width, width), 1
        )
        plain, turned = split(value), split(value.T)
        left_new = DECAY * left[slot] + (1.0 - DECAY) * product(plain, turned)
        right_new = DECAY * right[slot] + (1.0 - DECAY) * product(turned, plain)
        left_out[slot] = left_new
        right_out[slot] = right_new
        first, second = Root(left_new, eye), Root(right_new, eye)
        moved = product(split(product(first.factor, plain)), second.factor)
        for step in range(1, ITERS):
            first.advance()
            second.advance()
            if slot == 1 and step == 1:
                gather_half(0)
            moved = product(split(product(first.factor, split(moved))), second.factor)
        direction = (first.gain * second.gain) * moved
        count = 1.0 / (width * width)
        ratio = jnp.sqrt(total(value * value) * count) / jnp.sqrt(
            total(direction * direction) * count + 1e-06
        )
        ready[...] = (direction * ratio).astype(BF16).reshape(ready.shape)

        @pl.loop(1, n)
        def _(k):
            home_copy(slot, k).start()

        home[me] = ready[me]

    results = [
        pltpu.make_async_copy(left_out, ln_ref, local.at[3]),
        pltpu.make_async_copy(right_out, rn_ref, local.at[4]),
        pltpu.make_async_copy(gather0, upd_ref.at[pl.ds(0, HALF), me], local.at[5]),
        pltpu.make_async_copy(gather1, upd_ref.at[pl.ds(HALF, HALF), me], local.at[6]),
    ]
    for each in results[:3]:
        each.start()
    gather_half(1)
    results[3].start()

    @pl.loop(1, n)
    def _(k):
        part_copy(k).wait_send()
        for slot in range(2):
            slot_copy(slot, k).wait_send()
            home_copy(slot, k).wait_send()

    for each in results:
        each.wait()

    @pl.loop(1, n)
    def _(k):
        for half in range(2):
            gather_copy(half, k).wait()


def order_kernel(own_ref, upd_ref, ln_ref, rn_ref, out_ref, lo_ref, ro_ref, sem):
    blocks = own_ref.shape[0]
    _, places = ranks_of([own_ref[b] for b in range(blocks)])
    copies = [
        pltpu.make_async_copy(ln_ref, lo_ref, sem.at[blocks]),
        pltpu.make_async_copy(rn_ref, ro_ref, sem.at[blocks + 1]),
    ]
    copies += [
        pltpu.make_async_copy(upd_ref.at[places[b]], out_ref.at[b], sem.at[b])
        for b in range(blocks)
    ]
    for each in copies:
        each.start()
    for each in copies:
        each.wait()


def local(side, grad_parts, owner_list, left_stats, right_stats):
    n = side * side
    _, blocks, width, _ = grad_parts.shape
    owners = owner_list[:, 0]
    tiles = (blocks, n, ROWS, width)
    pair = (2, width, width)
    vmem = pltpu.VMEM
    anywhere = pl.BlockSpec(memory_space=pl.ANY)
    scalars = pl.BlockSpec(memory_space=pltpu.SMEM)
    piece = (n, ROWS, width)
    shapes = (
        jax.ShapeDtypeStruct(tiles, BF16),
        jax.ShapeDtypeStruct(pair, F32),
        jax.ShapeDtypeStruct(pair, F32),
    )
    update, left_new, right_new = pl.pallas_call(
        functools.partial(kernel, side),
        out_shape=shapes,
        in_specs=[scalars] + [anywhere] * 3,
        out_specs=(anywhere,) * 3,
        scratch_shapes=[
            vmem((n, blocks, ROWS, width), BF16),
            vmem((blocks, ROWS, width), F32),
            vmem(piece, F32),
            vmem(piece, F32),
            vmem(piece, F32),
            vmem(piece, F32),
            vmem(pair, F32),
            vmem(pair, F32),
            vmem(pair, F32),
            vmem(pair, F32),
            vmem(piece, BF16),
            vmem(piece, BF16),
            vmem(piece, BF16),
            vmem(piece, BF16),
            vmem((HALF, ROWS, width), BF16),
            vmem((HALF, ROWS, width), BF16),
            pltpu.SMEM((blocks,), jnp.int32),
            pltpu.SMEM((blocks,), jnp.int32),
            pltpu.SMEM((2, n), jnp.int32),
            pltpu.SemaphoreType.DMA((7, n)),
            pltpu.SemaphoreType.DMA((7, n)),
            pltpu.SemaphoreType.DMA((7,)),
        ],
        compiler_params=pltpu.CompilerParams(
            collective_id=0, has_side_effects=True, vmem_limit_bytes=40 * 1024 * 1024
        ),
    )(
        owners,
        grad_parts.reshape(tiles),
        left_stats.reshape(pair),
        right_stats.reshape(pair),
    )
    update, left_new, right_new = pl.pallas_call(
        order_kernel,
        out_shape=shapes,
        in_specs=[scalars] + [anywhere] * 3,
        out_specs=(anywhere,) * 3,
        scratch_shapes=[pltpu.SemaphoreType.DMA((blocks + 2,))],
    )(owners, update, left_new, right_new)
    return (
        update.reshape(blocks, width, width),
        left_new.reshape(left_stats.shape),
        right_new.reshape(right_stats.shape),
    )


def solution(mesh):
    side = int(round(mesh.shape["dp"] ** 0.5))
    return jax.shard_map(
        functools.partial(local, side),
        mesh=mesh,
        in_specs=(
            P("dp", "shard", None, None),
            P("shard", None),
            P("dp", "shard", None, None, None),
            P("dp", "shard", None, None, None),
        ),
        out_specs=(
            P("shard", None, None),
            P("dp", "shard", None, None, None),
            P("dp", "shard", None, None, None),
        ),
        check_vma=False,
    )
```

time: 247 us -> 159 us (0.64)
  the two profiles are of different devices: /device:TPU:1 before, /device:TPU:480 now
where the time goes in v1:
time: 159 us; the launch traced here: 158 us
  Pallas kernels  151 us (95%)
  local copies, waits for them, and re-layouts  6.88 us (4%)
    pallas_call x1, Pallas kernels, local(): pl.pallas_call(order_kernel, out_shape=shapes, in_specs=[scalars] + [anyw...  81.3 us
    pallas_call x1, Pallas kernels, local(): pl.pallas_call(functools.partial(kernel, side), out_shape=shapes, in_spec...  69.5 us
    unnamed x14, local copies, waits for them, and re-layouts  6.88 us

profile of v1, /device:TPU:480, one launch (start us, length us, event | category | flops | bytes accessed | tf_op | source)
XLA Modules:
  0.0 158.3 jit_solution(9266799007328108322)
XLA Ops:
  0.6 0.0 copy-start
  0.6 1.4 copy-done
  2.0 0.0 copy-start.2
  2.0 1.0 copy-done.2
  3.1 0.0 copy-start.3
  3.1 1.0 copy-done.3
  4.1 0.0 copy-start.6
  4.1 0.7 copy-done.6
  4.8 69.5 %shard_map.67 = (bf16[12,16,16,256]{3,2,1,0:T(8,128)(2,1)S(1)}, f32[2,256,256]{2,1,0:T(8,128)S(1)}, f32[2,256,256]{2,1,0:T(8,128)S(1)}) custom-call(s32[12]{0:T(128)S(1)} %bitcast.11, bf16[12,16,16,256]{3,2,1,0:T(8,128)(2,1)S(1)} %bitcast.7, f32[2,256,256]{2,1,0:T(8,128)S(1)} %bitcast.8, f32[2,256,256]{2,1,0:T(8,128)S(1)} %bitcast.9), custom_call_target="tpu_custom_call" | custom-call | tf_op jit(solution)/shard_map/pallas_call | solution.py:291
  74.3 0.0 copy-start.1
  74.3 1.1 copy-done.1
  75.4 0.0 copy-start.4
  75.4 0.8 copy-done.4
  76.2 0.0 copy-start.5
  76.2 0.8 copy-done.5
  77.0 81.3 %shard_map.68 = (bf16[12,16,16,256]{3,2,1,0:T(8,128)(2,1)}, f32[2,256,256]{2,1,0:T(8,128)}, f32[2,256,256]{2,1,0:T(8,128)}) custom-call(s32[12]{0:T(128)} %bitcast.10, bf16[12,16,16,256]{3,2,1,0:T(8,128)(2,1)} %copy-done.1, f32[2,256,256]{2,1,0:T(8,128)} %copy-done.4, f32[2,256,256]{2,1,0:T(8,128)} %copy-done.5), custom_call_target="tpu_custom_call" | custom-call | tf_op jit(solution)/shard_map/pallas_call | solution.py:329
Async XLA Ops:
  0.6 1.4 copy-start
  2.0 1.0 copy-start.2
  3.1 1.0 copy-start.3
  4.1 0.7 copy-start.6
  74.3 1.1 copy-start.1
  75.4 0.8 copy-start.4
  76.2 0.8 copy-start.5

commit v2 on v1

--- a/solution.py
+++ b/solution.py
@@ -11,6 +11,7 @@
 DECAY = 0.9
 RIDGE = 0.01
 ROWS = 16
+VMEM_BYTES = 56 * 1024 * 1024
 HALF = 6
 BF16, F32 = jnp.bfloat16, jnp.float32
 MESH = pl.DeviceIdType.MESH
@@ -256,21 +257,23 @@
             gather_copy(half, k).wait()
 
 
-def order_kernel(own_ref, upd_ref, ln_ref, rn_ref, out_ref, lo_ref, ro_ref, sem):
+def order_kernel(
+    own_ref, upd_ref, ln_ref, rn_ref, out_ref, lo_ref, ro_ref, upd, left, right, into, out
+):
     blocks = own_ref.shape[0]
     _, places = ranks_of([own_ref[b] for b in range(blocks)])
-    copies = [
-        pltpu.make_async_copy(ln_ref, lo_ref, sem.at[blocks]),
-        pltpu.make_async_copy(rn_ref, ro_ref, sem.at[blocks + 1]),
-    ]
-    copies += [
-        pltpu.make_async_copy(upd_ref.at[places[b]], out_ref.at[b], sem.at[b])
-        for b in range(blocks)
-    ]
-    for each in copies:
-        each.start()
-    for each in copies:
-        each.wait()
+    moves = [
+        (upd_ref.at[places[b]], upd.at[b], out_ref.at[b]) for b in range(blocks)
+    ] + [(ln_ref, left, lo_ref), (rn_ref, right, ro_ref)]
+    reads = [pltpu.make_async_copy(m[0], m[1], into.at[i]) for i, m in enumerate(moves)]
+    writes = [pltpu.make_async_copy(m[1], m[2], out.at[i]) for i, m in enumerate(moves)]
+    for read in reads:
+        read.start()
+    for read, write in zip(reads, writes):
+        read.wait()
+        write.start()
+    for write in writes:
+        write.wait()
 
 
 def local(side, grad_parts, owner_list, left_stats, right_stats):
@@ -291,7 +294,7 @@
     update, left_new, right_new = pl.pallas_call(
         functools.partial(kernel, side),
         out_shape=shapes,
-        in_specs=[scalars] + [anywhere] * 3,
+        in_specs=[scalars] + [pl.BlockSpec(memory_space=pltpu.HBM)] * 3,
         out_specs=(anywhere,) * 3,
         scratch_shapes=[
             vmem((n, blocks, ROWS, width), BF16),
@@ -318,7 +321,7 @@
             pltpu.SemaphoreType.DMA((7,)),
         ],
         compiler_params=pltpu.CompilerParams(
-            collective_id=0, has_side_effects=True, vmem_limit_bytes=40 * 1024 * 1024
+            collective_id=0, has_side_effects=True, vmem_limit_bytes=VMEM_BYTES
         ),
     )(
         owners,
@@ -331,7 +334,14 @@
         out_shape=shapes,
         in_specs=[scalars] + [anywhere] * 3,
         out_specs=(anywhere,) * 3,
-        scratch_shapes=[pltpu.SemaphoreType.DMA((blocks + 2,))],
+        scratch_shapes=[
+            vmem(tiles, BF16),
+            vmem(pair, F32),
+            vmem(pair, F32),
+            pltpu.SemaphoreType.DMA((blocks + 2,)),
+            pltpu.SemaphoreType.DMA((blocks + 2,)),
+        ],
+        compiler_params=pltpu.CompilerParams(vmem_limit_bytes=VMEM_BYTES),
     )(owners, update, left_new, right_new)
     return (
         update.reshape(blocks, width, width),

time: 159 us -> 74.3 us (0.47)
  Pallas kernels: 151 us -> 73.3 us
  local copies, waits for them, and re-layouts: 6.88 us -> 0 us
    pallas_call x1, Pallas kernels: 81.3 us -> 3.54 us  [local(): pl.pallas_call(order_kernel, out_shape=shapes, in_specs=[scalars] + [anyw...]
    unnamed x14 -> x0, local copies, waits for them, and re-layouts: 6.88 us -> none
where the time goes in v2:
time: 74.3 us; the launch traced here: 73.9 us
  Pallas kernels  73.3 us (99%)
    pallas_call x1, Pallas kernels, local(): pl.pallas_call(functools.partial(kernel, side), out_shape=shapes, in_spec...  69.8 us
    pallas_call x1, Pallas kernels, local(): pl.pallas_call(order_kernel, out_shape=shapes, in_specs=[scalars] + [anyw...  3.54 us

profile of v2, /device:TPU:480, one launch (start us, length us, event | category | flops | bytes accessed | tf_op | source)
XLA Modules:
  0.0 73.9 jit_solution(5107659366831287189)
XLA Ops:
  0.6 69.8 %shard_map.67 = (bf16[12,16,16,256]{3,2,1,0:T(8,128)(2,1)}, f32[2,256,256]{2,1,0:T(8,128)}, f32[2,256,256]{2,1,0:T(8,128)}) custom-call(s32[12]{0:T(128)} %bitcast.10, bf16[12,16,16,256]{3,2,1,0:T(8,128)(2,1)} %bitcast.7, f32[2,256,256]{2,1,0:T(8,128)} %bitcast.8, f32[2,256,256]{2,1,0:T(8,128)} %bitcast.9), custom_call_target="tpu_custom_call" | custom-call | tf_op jit(solution)/shard_map/pallas_call | solution.py:294
  70.4 3.5 %shard_map.68 = (bf16[12,16,16,256]{3,2,1,0:T(8,128)(2,1)}, f32[2,256,256]{2,1,0:T(8,128)}, f32[2,256,256]{2,1,0:T(8,128)}) custom-call(s32[12]{0:T(128)} %bitcast.11, bf16[12,16,16,256]{3,2,1,0:T(8,128)(2,1)} %get-tuple-element.9.upd_ref, f32[2,256,256]{2,1,0:T(8,128)} %get-tuple-element.10.ln_ref, f32[2,256,256]{2,1,0:T(8,128)} %get-tuple-element.11.rn_ref), custom_call_target="tpu_custom_call" | custom-call | tf_op jit(solution)/shard_map/pallas_call | solution.py:332

commit v3 on v2

--- a/solution.py
+++ b/solution.py
@@ -79,17 +79,27 @@
 
 def kernel(
     side, own_ref, g_ref, ls_ref, rs_ref, upd_ref, ln_ref, rn_ref,
-    parts, acc, picked0, picked1, grad0, grad1, left, right, left_out, right_out,
-    ready0, ready1, home0, home1, gather0, gather1,
-    owner_at, slot_at, block_at, send, recv, local,
+    parts, relay, sums, second, relay2, acc, picked0, picked1, grad0, grad1,
+    left, right, left_out, right_out, ready0, ready1, home0, home1, gathered,
+    owner_at, slot_at, block_at,
+    send_a, recv_a, send_b, recv_b, send_d, recv_d, send, recv, local,
 ):
     n = side * side
     blocks = own_ref.shape[0]
     me = lax.axis_index("dp")
     row, col = me // side, me % side
+    chunk = HALF // 2
 
     def peer(k):
         return ((row + k // side) % side) * side + (col + k % side) % side
+
+    def place(kind, du, dv):
+        dy, dx = (dv, du) if kind == 0 else (du, dv)
+        return ((row + dy + side) % side) * side + (col + dx + side) % side
+
+    def line(kind, du, dv):
+        at = [(c + d + side) % side for c, d in zip((col, row) if kind == 0 else (row, col), (du, dv))]
+        return at
 
     barrier = pltpu.get_barrier_semaphore()
 
@@ -99,37 +109,74 @@
 
     pl.semaphore_wait(barrier, n - 1)
 
-    def copy(stage, k, src, dst):
+    def remote(src, dst, sent, landed, to):
         return pltpu.make_async_remote_copy(
-            src_ref=src, dst_ref=dst, send_sem=send.at[stage, k], recv_sem=recv.at[stage, k],
-            device_id={"dp": peer(k)}, device_id_type=MESH,
+            src_ref=src, dst_ref=dst, send_sem=sent, recv_sem=landed,
+            device_id={"dp": to}, device_id_type=MESH,
         )
 
-    def part_copy(k):
-        return copy(A, k, g_ref.at[:, peer(k)], parts.at[k])
+    started = []
+
+    def begin(copy):
+        copy.start()
+        started.append(copy)
+
+    def raw_copy(kind, j, what, way):
+        step = 1 - 2 * way
+        rows = pl.ds(way * (side // 2), side // 2)
+        source = g_ref.at[pl.ds(kind * HALF + j * chunk, chunk)]
+        u = line(kind, 2 if what == 0 else step, 0)[0]
+        if what == 0:
+            src, dst = source.at[:, u, rows], relay.at[kind, j, way]
+        elif what == 1:
+            src, dst = source.at[:, u], parts.at[kind, j, way]
+        else:
+            src, dst = relay.at[kind, j, way], parts.at[kind, j, 2, :, rows]
+        at = (kind, j, what, way)
+        return remote(src, dst, send_a.at[at], recv_a.at[at], place(kind, step, 0))
+
+    def sum_copy(kind, j, what, way):
+        step = 1 - 2 * way
+        rows = pl.ds(way * (ROWS // 2), ROWS // 2)
+        v = line(kind, 0, 2 if what == 0 else step)[1]
+        if what == 0:
+            src, dst = sums.at[kind, j, v, :, rows], relay2.at[kind, j, way]
+        elif what == 1:
+            src, dst = sums.at[kind, j, v], second.at[kind, j, way]
+        else:
+            src, dst = relay2.at[kind, j, way], second.at[kind, j, 2, :, rows]
+        at = (kind, j, what, way)
+        return remote(src, dst, send_b.at[at], recv_b.at[at], place(kind, 0, step))
+
+    def direct(stage, k, src, dst):
+        return remote(src, dst, send.at[stage, k], recv.at[stage, k], peer(k))
 
     def slot_copy(slot, k):
-        return copy((B0, B1)[slot], k, (picked0, picked1)[slot].at[k], (grad0, grad1)[slot].at[me])
+        return direct(slot, k, (picked0, picked1)[slot].at[k], (grad0, grad1)[slot].at[me])
 
     def home_copy(slot, k):
-        return copy(
-            (C0, C1)[slot], k, (ready0, ready1)[slot].at[peer(k)], (home0, home1)[slot].at[me]
+        return direct(
+            2 + slot, k, (ready0, ready1)[slot].at[peer(k)], (home0, home1)[slot].at[me]
         )
 
-    def gather_copy(half, k):
-        return copy(
-            (D0, D1)[half], k, (gather0, gather1)[half], upd_ref.at[pl.ds(half * HALF, HALF), me]
-        )
-
-    @pl.loop(1, n)
-    def _(k):
-        part_copy(k).start()
-
-    mine = pltpu.make_async_copy(g_ref.at[:, me], parts.at[0], local.at[0])
-    mine.start()
+    kinds, ways = range(2), range(2)
+    for j in range(2):
+        for what in range(2):
+            for way in ways:
+                for kind in kinds:
+                    begin(raw_copy(kind, j, what, way))
+    mine = {}
+    for j in range(2):
+        for kind in kinds:
+            mine[kind, j] = pltpu.make_async_copy(
+                g_ref.at[pl.ds(kind * HALF + j * chunk, chunk), line(kind, 0, 0)[0]],
+                parts.at[kind, j, 3],
+                local.at[4 + 2 * kind + j],
+            )
+            mine[kind, j].start()
     stats = [
-        pltpu.make_async_copy(ls_ref, left, local.at[1]),
-        pltpu.make_async_copy(rs_ref, right, local.at[2]),
+        pltpu.make_async_copy(ls_ref, left, local.at[0]),
+        pltpu.make_async_copy(rs_ref, right, local.at[1]),
     ]
     for each in stats:
         each.start()
@@ -146,22 +193,46 @@
 
     @pl.loop(0, blocks)
     def _(p):
-        tests = [place == p for place in places]
+        tests = [at == p for at in places]
         owner_at[p] = chosen(tests, owners)
         slot_at[p] = chosen(tests, ranks)
 
-    used = [
-        chosen([(o == me) & (r == slot) for o, r in zip(owners, ranks)], [1] * blocks) > 0
-        for slot in range(2)
-    ]
-
-    mine.wait()
-    acc[...] = parts[0].astype(F32)
-
-    @pl.loop(1, n)
-    def _(k):
-        part_copy(k).wait_recv()
-        acc[...] += parts[k].astype(F32)
+    def mine_in(slot, first, last):
+        tests = [(o == me) & (r == slot) for o, r in zip(owners[first:last], ranks[first:last])]
+        return chosen(tests, [1] * (last - first)) > 0
+
+    for j in range(2):
+        for way in ways:
+            for kind in kinds:
+                raw_copy(kind, j, 0, way).wait_recv()
+                begin(raw_copy(kind, j, 2, way))
+    for j in range(2):
+        for kind in kinds:
+            for way in ways:
+                raw_copy(kind, j, 1, way).wait_recv()
+                raw_copy(kind, j, 2, way).wait_recv()
+            mine[kind, j].wait()
+
+            @pl.loop(0, side)
+            def _(v):
+                sums[kind, j, v] = sum(parts[kind, j, i, :, v].astype(F32) for i in range(side))
+
+            for what in range(2):
+                for way in ways:
+                    begin(sum_copy(kind, j, what, way))
+        for way in ways:
+            for kind in kinds:
+                sum_copy(kind, j, 0, way).wait_recv()
+                begin(sum_copy(kind, j, 2, way))
+    for j in range(2):
+        for kind in kinds:
+            for way in ways:
+                sum_copy(kind, j, 1, way).wait_recv()
+                sum_copy(kind, j, 2, way).wait_recv()
+            v = line(kind, 0, 0)[1]
+            acc[pl.ds(kind * HALF + j * chunk, chunk)] = sums[kind, j, v] + (
+                second[kind, j, 0] + second[kind, j, 1] + second[kind, j, 2]
+            )
 
     for slot in range(2):
         grad, picked = (grad0, grad1)[slot], (picked0, picked1)[slot]
@@ -176,7 +247,35 @@
     for each in stats:
         each.wait()
 
-    def gather_half(half):
+    def item_copy(half, kind, du, dv, over, cut=None):
+        at = half * HALF + kind * chunk
+        first, size = (0, chunk) if cut is None else cut
+        ref = gathered.at[pl.ds(at + first, size), place(kind, du, dv)]
+        seen = ((du - over[0]) % side, (dv - over[1]) % side)
+        lane = seen[0] * side + seen[1]
+        if cut is not None and first > 0:
+            lane = 0
+        sent = send_d.at[half, kind, (over[0] + 2 * over[1]) % 5 % 4, lane]
+        return remote(ref, ref, sent, recv_d.at[half, kind, lane], place(kind, *over))
+
+    def item_wait(half, kind, du, dv):
+        cuts = [None]
+        if dv == 0 and du % side == 2:
+            cuts = [(0, 2), (2, 1)]
+        for cut in cuts:
+            at = half * HALF + kind * chunk
+            first, size = (0, chunk) if cut is None else cut
+            ref = gathered.at[pl.ds(at + first, size), place(kind, du, dv)]
+            lane = (du % side) * side + dv % side
+            if cut is not None and first > 0:
+                lane = 0
+            remote(
+                ref, ref, send_d.at[half, kind, 0, 0], recv_d.at[half, kind, lane], place(kind, 0, 1)
+            ).wait_recv()
+
+    both = ((0, 1), (0, -1))
+
+    def gather_start(half):
         @pl.loop(1, n)
         def _(k):
             home_copy(half, k).wait_recv()
@@ -184,14 +283,51 @@
         for p in range(HALF):
             at = half * HALF + p
             if half == 0:
-                gather0[p] = home0[owner_at[at]]
+                gathered[at, me] = home0[owner_at[at]]
             else:
-                gather1[p] = jnp.where(slot_at[at] == 0, home0[owner_at[at]], home1[owner_at[at]])
-
-        @pl.loop(1, n)
-        def _(k):
-            gather_copy(half, k).start()
-
+                gathered[at, me] = jnp.where(
+                    slot_at[at] == 0, home0[owner_at[at]], home1[owner_at[at]]
+                )
+        for kind in kinds:
+            for over in ((1, 0), (-1, 0)):
+                begin(item_copy(half, kind, 0, 0, over))
+        for kind in kinds:
+            for over in both:
+                begin(item_copy(half, kind, 0, 0, over))
+
+    def gather_near(half):
+        for du in (-1, 1):
+            for kind in kinds:
+                item_wait(half, kind, du, 0)
+                begin(item_copy(half, kind, du, 0, (-du, 0), (0, 2) if du < 0 else (2, 1)))
+                for over in both:
+                    begin(item_copy(half, kind, du, 0, over))
+
+    def gather_far(half):
+        for kind in kinds:
+            item_wait(half, kind, 2, 0)
+            for over in both:
+                begin(item_copy(half, kind, 2, 0, over))
+
+    def gather_relay(half, first):
+        for du, dv in ((0, -1), (0, 1)) if first else ((-1, -1), (1, 1), (2, 1), (2, -1)):
+            for kind in kinds:
+                item_wait(half, kind, du, dv)
+                if (du, dv) in ((0, -1), (-1, -1), (1, 1), (2, 1)):
+                    begin(item_copy(half, kind, du, dv, (0, -dv)))
+
+    def gather_end(half):
+        for du, dv in ((-1, 1), (1, -1), (0, 2), (-1, 2), (1, 2), (2, 2)):
+            for kind in kinds:
+                item_wait(half, kind, du, dv)
+
+    def finish(half):
+        ref = pl.ds(half * HALF, HALF)
+        copy = pltpu.make_async_copy(gathered.at[ref], upd_ref.at[ref], local.at[8 + half])
+        copy.start()
+        return copy
+
+    results = []
     for slot in range(2):
         grad, ready, home = (grad0, grad1)[slot], (ready0, ready1)[slot], (home0, home1)[slot]
 
@@ -200,7 +336,12 @@
             slot_copy(slot, k).wait_recv()
 
         width = left.shape[1]
-        value = jnp.where(used[slot], grad[...].reshape(width, width), 0.0)
+        across = jnp.stack([grad[(i % side) * side + i // side] for i in range(n)])
+        value = jnp.where(
+            mine_in(slot, 0, HALF),
+            across,
+            jnp.where(mine_in(slot, HALF, blocks), grad[...], 0.0),
+        ).reshape(width, width)
         eye = lax.broadcasted_iota(jnp.int32, (width, width), 0) == lax.broadcasted_iota(
             jnp.int32, (width, width), 1
         )
@@ -209,15 +350,15 @@
         right_new = DECAY * right[slot] + (1.0 - DECAY) * product(turned, plain)
         left_out[slot] = left_new
         right_out[slot] = right_new
-        first, second = Root(left_new, eye), Root(right_new, eye)
-        moved = product(split(product(first.factor, plain)), second.factor)
+        first, other = Root(left_new, eye), Root(right_new, eye)
+        moved = product(split(product(first.factor, plain)), other.factor)
         for step in range(1, ITERS):
             first.advance()
-            second.advance()
-            if slot == 1 and step == 1:
-                gather_half(0)
-            moved = product(split(product(first.factor, split(moved))), second.factor)
-        direction = (first.gain * second.gain) * moved
+            other.advance()
+            if slot == 1:
+                (gather_start, gather_near, gather_far)[step - 1](0)
+            moved = product(split(product(first.factor, split(moved))), other.factor)
+        direction = (first.gain * other.gain) * moved
         count = 1.0 / (width * width)
         ratio = jnp.sqrt(total(value * value) * count) / jnp.sqrt(
             total(direction * direction) * count + 1e-06
@@ -230,31 +371,34 @@
 
         home[me] = ready[me]
 
-    results = [
-        pltpu.make_async_copy(left_out, ln_ref, local.at[3]),
-        pltpu.make_async_copy(right_out, rn_ref, local.at[4]),
-        pltpu.make_async_copy(gather0, upd_ref.at[pl.ds(0, HALF), me], local.at[5]),
-        pltpu.make_async_copy(gather1, upd_ref.at[pl.ds(HALF, HALF), me], local.at[6]),
+    results += [
+        pltpu.make_async_copy(left_out, ln_ref, local.at[2]),
+        pltpu.make_async_copy(right_out, rn_ref, local.at[3]),
     ]
-    for each in results[:3]:
+    for each in results:
         each.start()
-    gather_half(1)
-    results[3].start()
+    gather_relay(0, True)
+    gather_relay(0, False)
+    gather_start(1)
+    gather_near(1)
+    gather_far(1)
+    gather_end(0)
+    results.append(finish(0))
+    gather_relay(1, True)
+    gather_relay(1, False)
+    gather_end(1)
+    results.append(finish(1))
 
     @pl.loop(1, n)
     def _(k):
-        part_copy(k).wait_send()
         for slot in range(2):
             slot_copy(slot, k).wait_send()
             home_copy(slot, k).wait_send()
 
+    for each in started:
+        each.wait_send()
     for each in results:
         each.wait()
-
-    @pl.loop(1, n)
-    def _(k):
-        for half in range(2):
-            gather_copy(half, k).wait()
 
 
 def order_kernel(
@@ -281,6 +425,7 @@
     _, blocks, width, _ = grad_parts.shape
     owners = owner_list[:, 0]
     tiles = (blocks, n, ROWS, width)
+    chunk = HALF // 2
     pair = (2, width, width)
     vmem = pltpu.VMEM
     anywhere = pl.BlockSpec(memory_space=pl.ANY)
@@ -297,7 +442,11 @@
         in_specs=[scalars] + [pl.BlockSpec(memory_space=pltpu.HBM)] * 3,
         out_specs=(anywhere,) * 3,
         scratch_shapes=[
-            vmem((n, blocks, ROWS, width), BF16),
+            vmem((2, 2, side, chunk, side, ROWS, width), BF16),
+            vmem((2, 2, 2, chunk, side // 2, ROWS, width), BF16),
+            vmem((2, 2, side, chunk, ROWS, width), F32),
+            vmem((2, 2, 3, chunk, ROWS, width), F32),
+            vmem((2, 2, 2, chunk, ROWS // 2, width), F32),
             vmem((blocks, ROWS, width), F32),
             vmem(piece, F32),
             vmem(piece, F32),
@@ -311,21 +460,26 @@
             vmem(piece, BF16),
             vmem(piece, BF16),
             vmem(piece, BF16),
-            vmem((HALF, ROWS, width), BF16),
-            vmem((HALF, ROWS, width), BF16),
+            vmem(tiles, BF16),
             pltpu.SMEM((blocks,), jnp.int32),
             pltpu.SMEM((blocks,), jnp.int32),
             pltpu.SMEM((2, n), jnp.int32),
-            pltpu.SemaphoreType.DMA((7, n)),
-            pltpu.SemaphoreType.DMA((7, n)),
-            pltpu.SemaphoreType.DMA((7,)),
+            pltpu.SemaphoreType.DMA((2, 2, 3, 2)),
+            pltpu.SemaphoreType.DMA((2, 2, 3, 2)),
+            pltpu.SemaphoreType.DMA((2, 2, 3, 2)),
+            pltpu.SemaphoreType.DMA((2, 2, 3, 2)),
+            pltpu.SemaphoreType.DMA((2, 2, 4, n)),
+            pltpu.SemaphoreType.DMA((2, 2, n)),
+            pltpu.SemaphoreType.DMA((4, n)),
+            pltpu.SemaphoreType.DMA((4, n)),
+            pltpu.SemaphoreType.DMA((10,)),
         ],
         compiler_params=pltpu.CompilerParams(
             collective_id=0, has_side_effects=True, vmem_limit_bytes=VMEM_BYTES
         ),
     )(
         owners,
-        grad_parts.reshape(tiles),
+        grad_parts.reshape(blocks, side, side, ROWS, width),
         left_stats.reshape(pair),
         right_stats.reshape(pair),
     )

time: 74.3 us -> 83.3 us (1.12)
  Pallas kernels: 73.3 us -> 82.5 us
    pallas_call x1, Pallas kernels: 69.8 us -> 79 us  [local(): pl.pallas_call(functools.partial(kernel, side), out_shape=shapes, in_spec...]
where the time goes in v3:
time: 83.3 us; the launch traced here: 83.1 us
  Pallas kernels  82.5 us (99%)
    pallas_call x1, Pallas kernels, local(): pl.pallas_call(functools.partial(kernel, side), out_shape=shapes, in_spec...  79 us
    pallas_call x1, Pallas kernels, local(): pl.pallas_call(order_kernel, out_shape=shapes, in_specs=[scalars] + [anyw...  3.54 us

profile of v3, /device:TPU:480, one launch (start us, length us, event | category | flops | bytes accessed | tf_op | source)
XLA Modules:
  0.0 83.1 jit_solution(5612283976251584239)
XLA Ops:
  0.6 79.0 %shard_map.67 = (bf16[12,16,16,256]{3,2,1,0:T(8,128)(2,1)}, f32[2,256,256]{2,1,0:T(8,128)}, f32[2,256,256]{2,1,0:T(8,128)}) custom-call(s32[12]{0:T(128)} %bitcast.10, bf16[12,4,4,16,256]{4,3,2,1,0:T(8,128)(2,1)} %bitcast.7, f32[2,256,256]{2,1,0:T(8,128)} %bitcast.8, f32[2,256,256]{2,1,0:T(8,128)} %bitcast.9), custom_call_target="tpu_custom_call" | custom-call | tf_op jit(solution)/shard_map/pallas_call | solution.py:439
  79.6 3.5 %shard_map.68 = (bf16[12,16,16,256]{3,2,1,0:T(8,128)(2,1)}, f32[2,256,256]{2,1,0:T(8,128)}, f32[2,256,256]{2,1,0:T(8,128)}) custom-call(s32[12]{0:T(128)} %bitcast.11, bf16[12,16,16,256]{3,2,1,0:T(8,128)(2,1)} %get-tuple-element.9.upd_ref, f32[2,256,256]{2,1,0:T(8,128)} %get-tuple-element.10.ln_ref, f32[2,256,256]{2,1,0:T(8,128)} %get-tuple-element.11.rn_ref), custom_call_target="tpu_custom_call" | custom-call | tf_op jit(solution)/shard_map/pallas_call | solution.py:486

commit v4 on v1

v4 whole, which is shorter than its diff:
```python
import functools

import jax
import jax.numpy as jnp
from jax import lax
from jax.experimental import pallas as pl
from jax.experimental.pallas import tpu as pltpu
from jax.sharding import PartitionSpec as P

ITERS = 4
DECAY = 0.9
RIDGE = 0.01
ROWS = 16
VMEM_BYTES = 56 * 1024 * 1024
BF16, F32 = jnp.bfloat16, jnp.float32
MESH = pl.DeviceIdType.MESH
A, B0, B1, C0, C1, D0, D1 = range(7)


def split(value):
    high = value.astype(BF16)
    return high, (value - high.astype(F32)).astype(BF16)


def product(first, second):
    (ah, al), (bh, bl) = first, second
    return jnp.dot(
        jnp.concatenate([ah, ah, al], axis=1),
        jnp.concatenate([bh, bl, bh], axis=0),
        preferred_element_type=F32,
    )


def total(value):
    return jnp.sum(jnp.sum(value, axis=0, keepdims=True), axis=1, keepdims=True)


def ranks_of(owners):
    ranks = []
    for b, owner in enumerate(owners):
        rank = jnp.int32(0)
        for other in owners[:b]:
            rank = rank + jnp.where(other == owner, 1, 0)
        ranks.append(rank)
    firsts = sum(jnp.where(rank == 0, 1, 0) for rank in ranks)
    places, first, second = [], jnp.int32(0), firsts
    for rank in ranks:
        places.append(jnp.where(rank == 0, first, second))
        first = first + jnp.where(rank == 0, 1, 0)
        second = second + jnp.where(rank == 0, 0, 1)
    return ranks, places


def chosen(tests, values):
    return sum(jnp.where(test, value, 0) for test, value in zip(tests, values))


class Root:
    def __init__(self, statistic, eye):
        width = statistic.shape[0]
        shift = total(jnp.where(eye, statistic, 0.0)) * (RIDGE / width)
        shifted = statistic + jnp.where(eye, shift, 0.0)
        scale = 2.5 / jnp.sqrt(total(shifted * shifted) + 1e-06)
        self.eye = eye
        self.gain = jnp.sqrt(jnp.sqrt(scale))
        self.power = scale * shifted
        self.next_factor()

    def next_factor(self):
        self.factor = split(jnp.where(self.eye, 1.25, 0.0) - 0.25 * self.power)

    def advance(self):
        square = split(product(self.factor, self.factor))
        fourth = split(product(square, square))
        self.power = product(fourth, split(self.power))
        self.next_factor()


def peers(side):
    me = lax.axis_index("dp")
    row, col = me // side, me % side

    def peer(k):
        return ((row + k // side) % side) * side + (col + k % side) % side

    return me, peer


def greet(n, peer):
    barrier = pltpu.get_barrier_semaphore()

    @pl.loop(1, n)
    def _(k):
        pl.semaphore_signal(barrier, inc=1, device_id={"dp": peer(k)}, device_id_type=MESH)

    pl.semaphore_wait(barrier, n - 1)


def sum_kernel(side, own_ref, g_ref, grad, parts, acc, picked, block_at, send, recv, local):
    n = side * side
    blocks = own_ref.shape[0]
    me, peer = peers(side)
    greet(n, peer)

    def copy(stage, k, src, dst):
        return pltpu.make_async_remote_copy(
            src_ref=src, dst_ref=dst, send_sem=send.at[stage, k], recv_sem=recv.at[stage, k],
            device_id={"dp": peer(k)}, device_id_type=MESH,
        )

    def part_copy(k):
        return copy(0, k, g_ref.at[:, peer(k)], parts.at[k])

    def slot_copy(k):
        return copy(1, k, picked.at[k], grad.at[:, me])

    @pl.loop(1, n)
    def _(k):
        part_copy(k).start()

    mine = pltpu.make_async_copy(g_ref.at[:, me], parts.at[0], local.at[0])
    mine.start()
    owners = [own_ref[b] for b in range(blocks)]
    ranks, _ = ranks_of(owners)

    @pl.loop(0, n)
    def _(k):
        to = peer(k)
        for slot in range(2):
            tests = [(o == to) & (r == slot) for o, r in zip(owners, ranks)]
            block_at[slot, k] = chosen(tests, range(blocks))

    mine.wait()
    acc[...] = parts[0].astype(F32)

    @pl.loop(1, n)
    def _(k):
        part_copy(k).wait_recv()
        acc[...] += parts[k].astype(F32)

    @pl.loop(1, n)
    def _(k):
        for slot in range(2):
            picked[k, slot] = acc[block_at[slot, k]]
        slot_copy(k).start()

    for slot in range(2):
        picked[0, slot] = acc[block_at[slot, 0]]
    own = pltpu.make_async_copy(picked.at[0], grad.at[:, me], local.at[1])
    own.start()

    @pl.loop(1, n)
    def _(k):
        part_copy(k).wait_send()

    own.wait()

    @pl.loop(1, n)
    def _(k):
        slot_copy(k).wait()


def root_kernel(own_ref, grad_ref, left, right, ready, left_out, right_out):
    blocks = own_ref.shape[0]
    width = left.shape[1]
    me = lax.axis_index("dp")
    owners = [own_ref[b] for b in range(blocks)]
    ranks, _ = ranks_of(owners)
    eye = lax.broadcasted_iota(jnp.int32, (width, width), 0) == lax.broadcasted_iota(
        jnp.int32, (width, width), 1
    )
    slots = []
    for slot in range(2):
        used = chosen([(o == me) & (r == slot) for o, r in zip(owners, ranks)], [1] * blocks) > 0
        value = jnp.where(used, grad_ref[slot].reshape(width, width), 0.0)
        plain, turned = split(value), split(value.T)
        left_new = DECAY * left[slot] + (1.0 - DECAY) * product(plain, turned)
        right_new = DECAY * right[slot] + (1.0 - DECAY) * product(turned, plain)
        left_out[slot] = left_new
        right_out[slot] = right_new
        slots.append((value, plain, Root(left_new, eye), Root(right_new, eye)))
    moved = [split(product(first.factor, plain)) for _, plain, first, _ in slots]
    moved = [product(m, s[3].factor) for m, s in zip(moved, slots)]
    for step in range(1, ITERS):
        roots = [root for s in slots for root in s[2:]]
        squares = [split(product(r.factor, r.factor)) for r in roots]
        fourths = [split(product(q, q)) for q in squares]
        for root, fourth in zip(roots, fourths):
            root.power = product(fourth, split(root.power))
            root.next_factor()
        moved = [split(product(s[2].factor, split(m))) for m, s in zip(moved, slots)]
        moved = [product(m, s[3].factor) for m, s in zip(moved, slots)]
    for slot, (value, _, first, second) in enumerate(slots):
        direction = (first.gain * second.gain) * moved[slot]
        count = 1.0 / (width * width)
        ratio = jnp.sqrt(total(value * value) * count) / jnp.sqrt(
            total(direction * direction) * count + 1e-06
        )
        ready[:, slot] = (direction * ratio).astype(BF16).reshape(-1, ROWS, width)


def spread_kernel(side, own_ref, ready, upd_ref, home, gather, owner_at, slot_at, send, recv, local):
    n = side * side
    blocks = own_ref.shape[0]
    me, peer = peers(side)
    greet(n, peer)

    def copy(stage, k, src, dst):
        return pltpu.make_async_remote_copy(
            src_ref=src, dst_ref=dst, send_sem=send.at[stage, k], recv_sem=recv.at[stage, k],
            device_id={"dp": peer(k)}, device_id_type=MESH,
        )

    def home_copy(k):
        return copy(0, k, ready.at[peer(k)], home.at[me])

    def gather_copy(k):
        return copy(1, k, gather, upd_ref.at[:, me])

    @pl.loop(1, n)
    def _(k):
        home_copy(k).start()

    mine = pltpu.make_async_copy(ready.at[me], home.at[me], local.at[0])
    mine.start()
    owners = [own_ref[b] for b in range(blocks)]
    ranks, _ = ranks_of(owners)
    for b in range(blocks):
        owner_at[b] = owners[b]
        slot_at[b] = jnp.where(ranks[b] == 0, 0, 1)
    mine.wait()

    @pl.loop(1, n)
    def _(k):
        home_copy(k).wait_recv()

    for b in range(blocks):
        gather[b] = home[owner_at[b], slot_at[b]]

    @pl.loop(1, n)
    def _(k):
        gather_copy(k).start()

    own = pltpu.make_async_copy(gather, upd_ref.at[:, me], local.at[1])
    own.start()

    @pl.loop(1, n)
    def _(k):
        home_copy(k).wait_send()

    own.wait()

    @pl.loop(1, n)
    def _(k):
        gather_copy(k).wait()


def local(side, grad_parts, owner_list, left_stats, right_stats):
    n = side * side
    _, blocks, width, _ = grad_parts.shape
    owners = owner_list[:, 0]
    tiles = (blocks, n, ROWS, width)
    pair = (2, width, width)
    vmem = pltpu.VMEM
    anywhere = pl.BlockSpec(memory_space=pl.ANY)
    scalars = pl.BlockSpec(memory_space=pltpu.SMEM)
    piece = (n, ROWS, width)
    dma = pltpu.SemaphoreType.DMA
    grad = pl.pallas_call(
        functools.partial(sum_kernel, side),
        out_shape=jax.ShapeDtypeStruct((2,) + piece, F32),
        in_specs=[scalars, anywhere],
        out_specs=anywhere,
        scratch_shapes=[
            vmem((n, blocks, ROWS, width), BF16),
            vmem((blocks, ROWS, width), F32),
            vmem((n, 2, ROWS, width), F32),
            pltpu.SMEM((2, n), jnp.int32),
            dma((2, n)),
            dma((2, n)),
            dma((2,)),
        ],
        compiler_params=pltpu.CompilerParams(
            collective_id=0, has_side_effects=True, vmem_limit_bytes=VMEM_BYTES
        ),
    )(owners, grad_parts.reshape(tiles))
    ready, left_new, right_new = pl.pallas_call(
        root_kernel,
        out_shape=(
            jax.ShapeDtypeStruct((n, 2, ROWS, width), BF16),
            jax.ShapeDtypeStruct(pair, F32),
            jax.ShapeDtypeStruct(pair, F32),
        ),
        in_specs=[scalars] + [pl.BlockSpec(memory_space=vmem)] * 3,
        out_specs=(pl.BlockSpec(memory_space=vmem),) * 3,
        compiler_params=pltpu.CompilerParams(vmem_limit_bytes=VMEM_BYTES),
    )(owners, grad, left_stats.reshape(pair), right_stats.reshape(pair))
    update = pl.pallas_call(
        functools.partial(spread_kernel, side),
        out_shape=jax.ShapeDtypeStruct(tiles, BF16),
        in_specs=[scalars, anywhere],
        out_specs=anywhere,
        scratch_shapes=[
            vmem((n, 2, ROWS, width), BF16),
            vmem((blocks, ROWS, width), BF16),
            pltpu.SMEM((blocks,), jnp.int32),
            pltpu.SMEM((blocks,), jnp.int32),
            dma((2, n)),
            dma((2, n)),
            dma((2,)),
        ],
        compiler_params=pltpu.CompilerParams(
            collective_id=1, has_side_effects=True, vmem_limit_bytes=VMEM_BYTES
        ),
    )(owners, ready)
    return (
        update.reshape(blocks, width, width),
        left_new.reshape(left_stats.shape),
        right_new.reshape(right_stats.shape),
    )


def solution(mesh):
    side = int(round(mesh.shape["dp"] ** 0.5))
    return jax.shard_map(
        functools.partial(local, side),
        mesh=mesh,
        in_specs=(
            P("dp", "shard", None, None),
            P("shard", None),
            P("dp", "shard", None, None, None),
            P("dp", "shard", None, None, None),
        ),
        out_specs=(
            P("shard", None, None),
            P("dp", "shard", None, None, None),
            P("dp", "shard", None, None, None),
        ),
        check_vma=False,
    )
```

time: 159 us -> 82.7 us (0.52)
  Pallas kernels: 151 us -> 78 us
  local copies, waits for them, and re-layouts: 6.88 us -> 2.65 us
    pallas_call x2 -> x3, Pallas kernels: 151 us -> 78 us  [the longest x1 38.7 us: local(): pl.pallas_call(functools.partial(sum_kernel, side), out_shape=jax.ShapeDt...]
    unnamed x14 -> x1, local copies, waits for them, and re-layouts: 6.88 us -> 2.65 us
where the time goes in v4:
time: 82.7 us; the launch traced here: 81.3 us
  Pallas kernels  78 us (94%)
  local copies, waits for them, and re-layouts  2.65 us (3%)
    pallas_call x1, Pallas kernels, local(): pl.pallas_call(functools.partial(sum_kernel, side), out_shape=jax.ShapeDt...  38.7 us
    pallas_call x1, Pallas kernels, local(): pl.pallas_call(functools.partial(spread_kernel, side), out_shape=jax.Shap...  30.2 us
    pallas_call x1, Pallas kernels, local(): pl.pallas_call(root_kernel, out_shape=(jax.ShapeDtypeStruct((n, 2, ROWS,...  9.09 us
    unnamed x1, local copies, waits for them, and re-layouts  2.65 us

profile of v4, /device:TPU:480, one launch (start us, length us, event | category | flops | bytes accessed | tf_op | source)
XLA Modules:
  0.0 81.3 jit_solution(6782288948920575200)
XLA Ops:
  0.6 38.7 %shard_map.67.grad_ref = f32[2,16,16,256]{3,2,1,0:T(8,128)} custom-call(s32[12]{0:T(128)} %bitcast.11, bf16[12,16,16,256]{3,2,1,0:T(8,128)(2,1)} %bitcast.8), custom_call_target="tpu_custom_call" | custom-call | tf_op jit(solution)/shard_map/pallas_call | solution.py:269
  39.4 9.1 %shard_map.68 = (bf16[16,2,16,256]{3,2,1,0:T(8,128)(2,1)}, f32[2,256,256]{2,1,0:T(8,128)}, f32[2,256,256]{2,1,0:T(8,128)}) custom-call(s32[12]{0:T(128)} %bitcast.12, f32[2,16,16,256]{3,2,1,0:T(8,128)} %shard_map.67.grad_ref, f32[2,256,256]{2,1,0:T(8,128)} %bitcast.9, f32[2,256,256]{2,1,0:T(8,128)} %bitcast.10), custom_call_target="tpu_custom_call" | custom-call | tf_op jit(solution)/shard_map/pallas_call | solution.py:287
  48.4 30.2 %shard_map.69 = bf16[12,16,16,256]{3,2,1,0:T(8,128)(2,1)} custom-call(s32[12]{0:T(128)} %bitcast.13, bf16[16,2,16,256]{3,2,1,0:T(8,128)(2,1)} %get-tuple-element.6.ready), custom_call_target="tpu_custom_call" | custom-call | tf_op jit(solution)/shard_map/pallas_call | solution.py:298
  78.6 2.7 %copy.8 = bf16[12,256,256]{2,1,0:T(8,128)(2,1)} copy(bf16[12,256,256]{2,1,0:T(8,128)(2,1)} %bitcast.7) | data formatting | bytes 3145728

commit v5 on v2

v5 whole, which is shorter than its diff:
```python
import functools

import jax
import jax.numpy as jnp
from jax import lax
from jax.experimental import pallas as pl
from jax.experimental.pallas import tpu as pltpu
from jax.sharding import PartitionSpec as P

ITERS = 4
DECAY = 0.9
RIDGE = 0.01
ROWS = 16
VMEM_BYTES = 56 * 1024 * 1024
HALF = 6
BF16, F32 = jnp.bfloat16, jnp.float32
MESH = pl.DeviceIdType.MESH


def split(value):
    high = value.astype(BF16)
    return high, (value - high.astype(F32)).astype(BF16)


def product(first, second):
    (ah, al), (bh, bl) = first, second
    return jnp.dot(
        jnp.concatenate([ah, ah, al], axis=1),
        jnp.concatenate([bh, bl, bh], axis=0),
        preferred_element_type=F32,
    )


def total(value):
    return jnp.sum(jnp.sum(value, axis=0, keepdims=True), axis=1, keepdims=True)


def ranks_of(owners):
    ranks, places, kinds = [], [], []
    for b, owner in enumerate(owners):
        rank = sum((jnp.where(other == owner, 1, 0) for other in owners[:b]), jnp.int32(0))
        later = sum((jnp.where(other == owner, 1, 0) for other in owners[b + 1 :]), jnp.int32(0))
        ranks.append(rank)
        kinds.append(jnp.where(rank > 0, 2, jnp.where(later > 0, 0, 1)))
    counts = [sum(jnp.where(kind == i, 1, 0) for kind in kinds) for i in range(2)]
    nexts = [jnp.int32(0), counts[0], counts[0] + counts[1]]
    for kind in kinds:
        places.append(jnp.where(kind == 0, nexts[0], jnp.where(kind == 1, nexts[1], nexts[2])))
        nexts = [at + jnp.where(kind == i, 1, 0) for i, at in enumerate(nexts)]
    return ranks, places


def chosen(tests, values):
    return sum(jnp.where(test, value, 0) for test, value in zip(tests, values))


class Root:
    def __init__(self, statistic, eye):
        width = statistic.shape[0]
        shift = total(jnp.where(eye, statistic, 0.0)) * (RIDGE / width)
        shifted = statistic + jnp.where(eye, shift, 0.0)
        scale = 2.5 / jnp.sqrt(total(shifted * shifted) + 1e-06)
        self.eye = eye
        self.gain = jnp.sqrt(jnp.sqrt(scale))
        self.power = scale * shifted
        self.next_factor()

    def next_factor(self):
        self.factor = split(jnp.where(self.eye, 1.25, 0.0) - 0.25 * self.power)

    def advance(self):
        square = split(product(self.factor, self.factor))
        fourth = split(product(square, square))
        self.power = product(fourth, split(self.power))
        self.next_factor()


def kernel(
    side, own_ref, g_ref, ls_ref, rs_ref, upd_ref, ln_ref, rn_ref,
    given, staged, parts0, parts1, acc0, acc1, picked0, picked1, grad0, grad1,
    left, right, left_out, right_out, ready0, ready1, home0, home1, lines0, lines1,
    block_at, owner_at, index_at,
    send, recv, send_line, recv_line, local,
):
    n = side * side
    blocks = own_ref.shape[0]
    width = left.shape[1]
    me = lax.axis_index("dp")
    row, col = me // side, me % side
    chunk = HALF // 2
    parts, acc, picked, grad = (parts0, parts1), (acc0, acc1), (picked0, picked1), (grad0, grad1)
    ready, home, lines = (ready0, ready1), (home0, home1), (lines0, lines1)

    def peer(k):
        return ((row + k // side) % side) * side + (col + k % side) % side

    def along(axis, k):
        if axis == 0:
            return row * side + (col + k) % side
        return ((row + k) % side) * side + col

    loads = [
        pltpu.make_async_copy(g_ref, given, local.at[0]),
        pltpu.make_async_copy(ls_ref, left, local.at[1]),
        pltpu.make_async_copy(rs_ref, right, local.at[2]),
    ]
    for load in loads:
        load.start()
    barrier = pltpu.get_barrier_semaphore()

    @pl.loop(1, n)
    def _(k):
        pl.semaphore_signal(barrier, inc=1, device_id={"dp": peer(k)}, device_id_type=MESH)

    owners = [own_ref[b] for b in range(blocks)]
    ranks, places = ranks_of(owners)

    @pl.loop(0, blocks)
    def _(p):
        tests = [at == p for at in places]
        block_at[p] = chosen(tests, range(blocks))
        owner_at[p] = chosen(tests, owners)

    def remote(src, dst, sent, landed, to):
        return pltpu.make_async_remote_copy(
            src_ref=src, dst_ref=dst, send_sem=sent, recv_sem=landed,
            device_id={"dp": to}, device_id_type=MESH,
        )

    def direct(what, half, k, src, dst):
        at = (2 * what + half, k)
        return remote(src, dst, send.at[at], recv.at[at], peer(k))

    def part_copy(half, k):
        return direct(
            0, half, k, staged.at[pl.ds(half * HALF, HALF), peer(k)], parts[half].at[k]
        )

    def slot_copy(half, k):
        return direct(1, half, k, picked[half].at[k], grad[half].at[me])

    def home_copy(half, k):
        return direct(2, half, k, ready[half].at[peer(k)], home[half].at[me])

    def line_copy(half, step, axis, k):
        at = (half, step, axis, k)
        held = lines[half].at[axis]
        if step == 0:
            src = dst = held.at[:, (col, row)[axis]]
            to = along(axis, k)
        else:
            src, dst, to = held, line_place(half, axis), along(1 - axis, k)
        return remote(src, dst, send_line.at[at], recv_line.at[at], to)

    def line_place(half, axis):
        ref = upd_ref.at[pl.ds(half * HALF + axis * chunk, chunk)]
        return ref.at[:, row] if axis == 0 else ref.at[:, :, col]

    loads[0].wait()
    for half in range(2):
        for p in range(half * HALF, (half + 1) * HALF):
            staged[p] = given[block_at[p]]
        if half == 0:
            pl.semaphore_wait(barrier, n - 1)

        @pl.loop(1, n)
        def _(k):
            part_copy(half, k).start()

    @pl.loop(0, n)
    def _(k):
        to = peer(k)
        for half in range(2):
            index = jnp.int32(0)
            for i in range(1, HALF):
                index = jnp.where(owner_at[half * HALF + i] == to, i, index)
            index_at[half, k] = index

    def mine(half, slot):
        tests = []
        for owner, rank, at in zip(owners, ranks, places):
            inside = (at < HALF) if half == 0 else (at >= HALF)
            tests.append((owner == me) & inside & ((rank == 0) if slot == 0 else (rank > 0)))
        return chosen(tests, [1] * blocks) > 0

    def to_owners(half):
        acc[half][...] = staged[pl.ds(half * HALF, HALF), me].astype(F32)

        @pl.loop(1, n)
        def _(k):
            part_copy(half, k).wait_recv()
            acc[half][...] += parts[half][k].astype(F32)

        @pl.loop(1, n)
        def _(k):
            picked[half][k] = acc[half][index_at[half, k]]
            slot_copy(half, k).start()

        grad[half][me] = acc[half][index_at[half, 0]]

    eye = lax.broadcasted_iota(jnp.int32, (width, width), 0) == lax.broadcasted_iota(
        jnp.int32, (width, width), 1
    )

    def solve(half, used, left_old, right_old, beside):
        @pl.loop(1, n)
        def _(k):
            slot_copy(half, k).wait_recv()

        value = jnp.where(used, grad[half][...].reshape(width, width), 0.0)
        plain, turned = split(value), split(value.T)
        left_new = DECAY * left_old + (1.0 - DECAY) * product(plain, turned)
        right_new = DECAY * right_old + (1.0 - DECAY) * product(turned, plain)
        if half == 0:
            left_out[0] = left_new
            right_out[0] = right_new
        else:
            for slot in range(2):
                here = mine(1, slot)
                for out, old, new in (
                    (left_out, left, left_new), (right_out, right, right_new)
                ):
                    rest = out[0] if slot == 0 else DECAY * old[1]
                    out[slot] = jnp.where(here, new, rest)
        first, second = Root(left_new, eye), Root(right_new, eye)
        moved = product(split(product(first.factor, plain)), second.factor)
        for step in range(1, ITERS):
            first.advance()
            second.advance()
            beside(step)
            moved = product(split(product(first.factor, split(moved))), second.factor)
        direction = (first.gain * second.gain) * moved
        count = 1.0 / (width * width)
        ratio = jnp.sqrt(total(value * value) * count) / jnp.sqrt(
            total(direction * direction) * count + 1e-06
        )
        ready[half][...] = (direction * ratio).astype(BF16).reshape(ready[half].shape)

        @pl.loop(1, n)
        def _(k):
            home_copy(half, k).start()

        home[half][me] = ready[half][me]

    def along_first(half):
        @pl.loop(1, n)
        def _(k):
            home_copy(half, k).wait_recv()

        for axis in range(2):
            for p in range(chunk):
                value = home[half][owner_at[half * HALF + axis * chunk + p]]
                lines[half][axis, p, (col, row)[axis]] = value
            for k in range(1, side):
                line_copy(half, 0, axis, k).start()

    rests = []

    def along_second(half):
        for axis in range(2):
            for k in range(1, side):
                line_copy(half, 0, axis, k).wait_recv()
            for k in range(1, side):
                line_copy(half, 1, axis, k).start()
            rest = pltpu.make_async_copy(
                lines[half].at[axis], line_place(half, axis), local.at[5 + 2 * half + axis]
            )
            rest.start()
            rests.append(rest)

    to_owners(0)
    loads[1].wait()
    loads[2].wait()

    def beside_first(step):
        if step == 2:
            to_owners(1)

    def beside_second(step):
        if step == 3:
            along_first(0)

    solve(0, mine(0, 0), left[0], right[0], beside_first)
    slot = jnp.where(mine(1, 1), 1, 0)
    used = mine(1, 0) | mine(1, 1)
    solve(1, used, left[slot], right[slot], beside_second)
    along_second(0)
    for ref, out, at in ((left_out, ln_ref, 3), (right_out, rn_ref, 4)):
        rest = pltpu.make_async_copy(ref, out, local.at[at])
        rest.start()
        rests.append(rest)
    along_first(1)
    along_second(1)

    @pl.loop(1, n)
    def _(k):
        for half in range(2):
            part_copy(half, k).wait_send()
            slot_copy(half, k).wait_send()
            home_copy(half, k).wait_send()

    for half in range(2):
        for axis in range(2):
            for k in range(1, side):
                line_copy(half, 0, axis, k).wait_send()
                line_copy(half, 1, axis, k).wait()
    for rest in rests:
        rest.wait()


def order_kernel(
    own_ref, upd_ref, ln_ref, rn_ref, out_ref, lo_ref, ro_ref, upd, left, right, into, out
):
    blocks = own_ref.shape[0]
    _, places = ranks_of([own_ref[b] for b in range(blocks)])
    moves = [
        (upd_ref.at[places[b]], upd.at[b], out_ref.at[b]) for b in range(blocks)
    ] + [(ln_ref, left, lo_ref), (rn_ref, right, ro_ref)]
    reads = [pltpu.make_async_copy(m[0], m[1], into.at[i]) for i, m in enumerate(moves)]
    writes = [pltpu.make_async_copy(m[1], m[2], out.at[i]) for i, m in enumerate(moves)]
    for read in reads:
        read.start()
    for read, write in zip(reads, writes):
        read.wait()
        write.start()
    for write in writes:
        write.wait()


def local(side, grad_parts, owner_list, left_stats, right_stats):
    n = side * side
    _, blocks, width, _ = grad_parts.shape
    owners = owner_list[:, 0]
    tiles = (blocks, n, ROWS, width)
    pair = (2, width, width)
    vmem = pltpu.VMEM
    anywhere = pl.BlockSpec(memory_space=pl.ANY)
    scalars = pl.BlockSpec(memory_space=pltpu.SMEM)
    piece = (n, ROWS, width)
    shapes = (
        jax.ShapeDtypeStruct((blocks, side, side, ROWS, width), BF16),
        jax.ShapeDtypeStruct(pair, F32),
        jax.ShapeDtypeStruct(pair, F32),
    )
    some = (HALF, ROWS, width)
    dma = pltpu.SemaphoreType.DMA
    update, left_new, right_new = pl.pallas_call(
        functools.partial(kernel, side),
        out_shape=shapes,
        in_specs=[scalars] + [anywhere] * 3,
        out_specs=(anywhere,) * 3,
        scratch_shapes=[vmem(tiles, BF16)] * 2
        + [vmem((n,) + some, BF16)] * 2
        + [vmem(some, F32)] * 2
        + [vmem(piece, F32)] * 4
        + [vmem(pair, F32)] * 4
        + [vmem(piece, BF16)] * 4
        + [vmem((2, HALF // 2, side, ROWS, width), BF16)] * 2
        + [
            pltpu.SMEM((blocks,), jnp.int32),
            pltpu.SMEM((blocks,), jnp.int32),
            pltpu.SMEM((2, n), jnp.int32),
            dma((6, n)),
            dma((6, n)),
            dma((2, 2, 2, side)),
            dma((2, 2, 2, side)),
            dma((9,)),
        ],
        compiler_params=pltpu.CompilerParams(
            collective_id=0, has_side_effects=True, vmem_limit_bytes=VMEM_BYTES
        ),
    )(
        owners,
        grad_parts.reshape(tiles),
        left_stats.reshape(pair),
        right_stats.reshape(pair),
    )
    update, left_new, right_new = pl.pallas_call(
        order_kernel,
        out_shape=shapes,
        in_specs=[scalars] + [anywhere] * 3,
        out_specs=(anywhere,) * 3,
        scratch_shapes=[
            vmem((blocks, side, side, ROWS, width), BF16),
            vmem(pair, F32),
            vmem(pair, F32),
            pltpu.SemaphoreType.DMA((blocks + 2,)),
            pltpu.SemaphoreType.DMA((blocks + 2,)),
        ],
        compiler_params=pltpu.CompilerParams(vmem_limit_bytes=VMEM_BYTES),
    )(owners, update, left_new, right_new)
    return (
        update.reshape(blocks, width, width),
        left_new.reshape(left_stats.shape),
        right_new.reshape(right_stats.shape),
    )


def solution(mesh):
    side = int(round(mesh.shape["dp"] ** 0.5))
    return jax.shard_map(
        functools.partial(local, side),
        mesh=mesh,
        in_specs=(
            P("dp", "shard", None, None),
            P("shard", None),
            P("dp", "shard", None, None, None),
            P("dp", "shard", None, None, None),
        ),
        out_specs=(
            P("shard", None, None),
            P("dp", "shard", None, None, None),
            P("dp", "shard", None, None, None),
        ),
        check_vma=False,
    )
```

time: 74.3 us -> 71.6 us (0.964)
  Pallas kernels: 73.3 us -> 70.8 us
    pallas_call x1, Pallas kernels: 69.8 us -> 67.1 us  [local(): pl.pallas_call(functools.partial(kernel, side), out_shape=shapes, in_spec...]
where the time goes in v5:
time: 71.6 us; the launch traced here: 71.4 us
  Pallas kernels  70.8 us (99%)
    pallas_call x1, Pallas kernels, local(): pl.pallas_call(functools.partial(kernel, side), out_shape=shapes, in_spec...  67.1 us
    pallas_call x1, Pallas kernels, local(): pl.pallas_call(order_kernel, out_shape=shapes, in_specs=[scalars] + [anyw...  3.69 us

profile of v5, /device:TPU:480, one launch (start us, length us, event | category | flops | bytes accessed | tf_op | source)
XLA Modules:
  0.0 71.4 jit_solution(11994938914697600820)
XLA Ops:
  0.6 67.1 %shard_map.67 = (bf16[12,4,4,16,256]{4,3,2,1,0:T(8,128)(2,1)}, f32[2,256,256]{2,1,0:T(8,128)}, f32[2,256,256]{2,1,0:T(8,128)}) custom-call(s32[12]{0:T(128)} %bitcast.10, bf16[12,16,16,256]{3,2,1,0:T(8,128)(2,1)} %bitcast.7, f32[2,256,256]{2,1,0:T(8,128)} %bitcast.8, f32[2,256,256]{2,1,0:T(8,128)} %bitcast.9), custom_call_target="tpu_custom_call" | custom-call | tf_op jit(solution)/shard_map/pallas_call | solution.py:347
  67.7 3.7 %shard_map.68 = (bf16[12,4,4,16,256]{4,3,2,1,0:T(8,128)(2,1)}, f32[2,256,256]{2,1,0:T(8,128)}, f32[2,256,256]{2,1,0:T(8,128)}) custom-call(s32[12]{0:T(128)} %bitcast.11, bf16[12,4,4,16,256]{4,3,2,1,0:T(8,128)(2,1)} %get-tuple-element.9.upd_ref, f32[2,256,256]{2,1,0:T(8,128)} %get-tuple-element.10.ln_ref, f32[2,256,256]{2,1,0:T(8,128)} %get-tuple-element.11.rn_ref), custom_call_target="tpu_custom_call" | custom-call | tf_op jit(solution)/shard_map/pallas_call | solution.py:378

commit v6 on v5

--- a/solution.py
+++ b/solution.py
@@ -75,12 +75,20 @@
         self.next_factor()
 
 
+DETOURS = (
+    ((1, 2), (1, -1), (0, -1)),
+    ((3, 2), (-1, -1), (0, -1)),
+    ((2, 1), (-1, 1), (-1, 0)),
+    ((2, 3), (-1, -1), (-1, 0)),
+)
+
+
 def kernel(
     side, own_ref, g_ref, ls_ref, rs_ref, upd_ref, ln_ref, rn_ref,
     given, staged, parts0, parts1, acc0, acc1, picked0, picked1, grad0, grad1,
     left, right, left_out, right_out, ready0, ready1, home0, home1, lines0, lines1,
-    block_at, owner_at, index_at,
-    send, recv, send_line, recv_line, local,
+    hop0, hop1, block_at, owner_at, index_at,
+    send_hop, recv_hop, send, recv, send_line, recv_line, local,
 ):
     n = side * side
     blocks = own_ref.shape[0]
@@ -90,6 +98,7 @@
     chunk = HALF // 2
     parts, acc, picked, grad = (parts0, parts1), (acc0, acc1), (picked0, picked1), (grad0, grad1)
     ready, home, lines = (ready0, ready1), (home0, home1), (lines0, lines1)
+    hops = (hop0, hop1)
 
     def peer(k):
         return ((row + k // side) % side) * side + (col + k % side) % side
@@ -136,6 +145,30 @@
             0, half, k, staged.at[pl.ds(half * HALF, HALF), peer(k)], parts[half].at[k]
         )
 
+    def at_steps(dy, dx):
+        return ((row + dy + side) % side) * side + (col + dx + side) % side
+
+    def hop_copy(half, i):
+        (dy, dx), via, _ = DETOURS[i]
+        src = staged.at[pl.ds(half * HALF, HALF), at_steps(dy, dx)]
+        at = (half, 0, i)
+        return remote(src, hops[half].at[i], send_hop.at[at], recv_hop.at[half, i], at_steps(*via))
+
+    def last_copy(half, i):
+        (dy, dx), _, last = DETOURS[i]
+        k = dy * side + dx
+        return remote(
+            hops[half].at[i], parts[half].at[k], send_hop.at[half, 1, i], recv.at[half, k],
+            at_steps(*last),
+        )
+
+    def send_on(half):
+        for i in range(len(DETOURS)):
+            hop_copy(half, i).wait_recv()
+            last_copy(half, i).start()
+
+    straight = [k for k in range(1, n) if (k // side, k % side) not in [d[0] for d in DETOURS]]
+
     def slot_copy(half, k):
         return direct(1, half, k, picked[half].at[k], grad[half].at[me])
 
@@ -149,12 +182,28 @@
             src = dst = held.at[:, (col, row)[axis]]
             to = along(axis, k)
         else:
-            src, dst, to = held, line_place(half, axis), along(1 - axis, k)
+            to = along(1 - axis, k)
+            if k == 2:
+                src, dst = held.at[pl.ds(0, 1)], line_place(half, axis, 0, 0, 1)
+            else:
+                src, dst = held, line_place(half, axis)
         return remote(src, dst, send_line.at[at], recv_line.at[at], to)
 
-    def line_place(half, axis):
-        ref = upd_ref.at[pl.ds(half * HALF + axis * chunk, chunk)]
-        return ref.at[:, row] if axis == 0 else ref.at[:, :, col]
+    def line_place(half, axis, step=0, first=0, size=chunk):
+        ref = upd_ref.at[pl.ds(half * HALF + axis * chunk + first, size)]
+        if axis == 0:
+            return ref.at[:, (row + step) % side]
+        return ref.at[:, :, (col + step) % side]
+
+    def line_pass(half, axis):
+        ref = line_place(half, axis, 1, 1, chunk - 1)
+        at = (half, 1, axis, 0)
+        return remote(ref, ref, send_line.at[at], recv_line.at[at], along(1 - axis, side - 1))
+
+    def pass_lines(half):
+        for axis in range(2):
+            line_copy(half, 1, axis, side - 1).wait_recv()
+            line_pass(half, axis).start()
 
     loads[0].wait()
     for half in range(2):
@@ -163,8 +212,9 @@
         if half == 0:
             pl.semaphore_wait(barrier, n - 1)
 
-        @pl.loop(1, n)
-        def _(k):
+        for i in range(len(DETOURS)):
+            hop_copy(half, i).start()
+        for k in straight:
             part_copy(half, k).start()
 
     @pl.loop(0, n)
@@ -268,7 +318,9 @@
             rest.start()
             rests.append(rest)
 
+    send_on(0)
     to_owners(0)
+    send_on(1)
     loads[1].wait()
     loads[2].wait()
 
@@ -290,20 +342,29 @@
         rest.start()
         rests.append(rest)
     along_first(1)
+    pass_lines(0)
     along_second(1)
+    pass_lines(1)
 
     @pl.loop(1, n)
     def _(k):
         for half in range(2):
-            part_copy(half, k).wait_send()
             slot_copy(half, k).wait_send()
             home_copy(half, k).wait_send()
 
     for half in range(2):
+        for k in straight:
+            part_copy(half, k).wait_send()
+        for i in range(len(DETOURS)):
+            hop_copy(half, i).wait_send()
+            last_copy(half, i).wait_send()
         for axis in range(2):
+            line_pass(half, axis).wait()
             for k in range(1, side):
                 line_copy(half, 0, axis, k).wait_send()
-                line_copy(half, 1, axis, k).wait()
+                line_copy(half, 1, axis, k).wait_send()
+                if k < side - 1:
+                    line_copy(half, 1, axis, k).wait_recv()
     for rest in rests:
         rest.wait()
 
@@ -356,10 +417,13 @@
         + [vmem(pair, F32)] * 4
         + [vmem(piece, BF16)] * 4
         + [vmem((2, HALF // 2, side, ROWS, width), BF16)] * 2
+        + [vmem((len(DETOURS),) + some, BF16)] * 2
         + [
             pltpu.SMEM((blocks,), jnp.int32),
             pltpu.SMEM((blocks,), jnp.int32),
             pltpu.SMEM((2, n), jnp.int32),
+            dma((2, 2, len(DETOURS))),
+            dma((2, len(DETOURS))),
             dma((6, n)),
             dma((6, n)),
             dma((2, 2, 2, side)),

time: 71.6 us -> 76.8 us (1.073); the launches traced: 71.4 us -> 75.7 us
  Pallas kernels: 70.8 us -> 75 us
    pallas_call x1, Pallas kernels: 67.1 us -> 71.4 us  [local(): pl.pallas_call(functools.partial(kernel, side), out_shape=shapes, in_spec...]
where the time goes in v6:
time: 76.8 us; the launch traced here: 75.7 us
  Pallas kernels  75 us (98%)
    pallas_call x1, Pallas kernels, local(): pl.pallas_call(functools.partial(kernel, side), out_shape=shapes, in_spec...  71.4 us
    pallas_call x1, Pallas kernels, local(): pl.pallas_call(order_kernel, out_shape=shapes, in_specs=[scalars] + [anyw...  3.69 us

profile of v6, /device:TPU:480, one launch (start us, length us, event | category | flops | bytes accessed | tf_op | source)
XLA Modules:
  0.0 75.7 jit_solution(9266591075261423548)
XLA Ops:
  0.6 71.4 %shard_map.67 = (bf16[12,4,4,16,256]{4,3,2,1,0:T(8,128)(2,1)}, f32[2,256,256]{2,1,0:T(8,128)}, f32[2,256,256]{2,1,0:T(8,128)}) custom-call(s32[12]{0:T(128)} %bitcast.10, bf16[12,16,16,256]{3,2,1,0:T(8,128)(2,1)} %bitcast.7, f32[2,256,256]{2,1,0:T(8,128)} %bitcast.8, f32[2,256,256]{2,1,0:T(8,128)} %bitcast.9), custom_call_target="tpu_custom_call" | custom-call | tf_op jit(solution)/shard_map/pallas_call | solution.py:408
  72.0 3.7 %shard_map.68 = (bf16[12,4,4,16,256]{4,3,2,1,0:T(8,128)(2,1)}, f32[2,256,256]{2,1,0:T(8,128)}, f32[2,256,256]{2,1,0:T(8,128)}) custom-call(s32[12]{0:T(128)} %bitcast.11, bf16[12,4,4,16,256]{4,3,2,1,0:T(8,128)(2,1)} %get-tuple-element.9.upd_ref, f32[2,256,256]{2,1,0:T(8,128)} %get-tuple-element.10.ln_ref, f32[2,256,256]{2,1,0:T(8,128)} %get-tuple-element.11.rn_ref), custom_call_target="tpu_custom_call" | custom-call | tf_op jit(solution)/shard_map/pallas_call | solution.py:442

commit v7 on v5

--- a/solution.py
+++ b/solution.py
@@ -99,6 +99,11 @@
             return row * side + (col + k) % side
         return ((row + k) % side) * side + col
 
+    core = lax.axis_index("shard") % 2
+
+    def turned_round(i):
+        return 1 + (i + me + core * (n // 2 - 1)) % (n - 1)
+
     loads = [
         pltpu.make_async_copy(g_ref, given, local.at[0]),
         pltpu.make_async_copy(ls_ref, left, local.at[1]),
@@ -163,9 +168,9 @@
         if half == 0:
             pl.semaphore_wait(barrier, n - 1)
 
-        @pl.loop(1, n)
-        def _(k):
-            part_copy(half, k).start()
+        @pl.loop(0, n - 1)
+        def _(i):
+            part_copy(half, turned_round(i)).start()
 
     @pl.loop(0, n)
     def _(k):
@@ -191,8 +196,9 @@
             part_copy(half, k).wait_recv()
             acc[half][...] += parts[half][k].astype(F32)
 
-        @pl.loop(1, n)
-        def _(k):
+        @pl.loop(0, n - 1)
+        def _(i):
+            k = turned_round(i)
             picked[half][k] = acc[half][index_at[half, k]]
             slot_copy(half, k).start()
 
@@ -236,9 +242,9 @@
         )
         ready[half][...] = (direction * ratio).astype(BF16).reshape(ready[half].shape)
 
-        @pl.loop(1, n)
-        def _(k):
-            home_copy(half, k).start()
+        @pl.loop(0, n - 1)
+        def _(i):
+            home_copy(half, turned_round(i)).start()
 
         home[half][me] = ready[half][me]
 
@@ -251,17 +257,23 @@
             for p in range(chunk):
                 value = home[half][owner_at[half * HALF + axis * chunk + p]]
                 lines[half][axis, p, (col, row)[axis]] = value
-            for k in range(1, side):
-                line_copy(half, 0, axis, k).start()
+        for i in range(side - 1):
+            for axis in range(2):
+                line_copy(half, 0, axis, line_turn(axis, i)).start()
 
     rests = []
+
+    def line_turn(axis, i):
+        return 1 + (i + row + col + core + axis) % (side - 1)
 
     def along_second(half):
         for axis in range(2):
             for k in range(1, side):
                 line_copy(half, 0, axis, k).wait_recv()
-            for k in range(1, side):
-                line_copy(half, 1, axis, k).start()
+        for i in range(side - 1):
+            for axis in range(2):
+                line_copy(half, 1, axis, line_turn(axis, i)).start()
+        for axis in range(2):
             rest = pltpu.make_async_copy(
                 lines[half].at[axis], line_place(half, axis), local.at[5 + 2 * half + axis]
             )

time: 71.6 us -> 71.5 us (level)
  no operation moved by 1% of the time
where the time goes in v7:
time: 71.5 us; the launch traced here: 71.1 us
  Pallas kernels  70.5 us (99%)
    pallas_call x1, Pallas kernels, local(): pl.pallas_call(functools.partial(kernel, side), out_shape=shapes, in_spec...  66.8 us
    pallas_call x1, Pallas kernels, local(): pl.pallas_call(order_kernel, out_shape=shapes, in_specs=[scalars] + [anyw...  3.69 us

profile of v7, /device:TPU:480, one launch (start us, length us, event | category | flops | bytes accessed | tf_op | source)
XLA Modules:
  0.0 71.1 jit_solution(10787767563415022486)
XLA Ops:
  0.6 66.8 %shard_map.67 = (bf16[12,4,4,16,256]{4,3,2,1,0:T(8,128)(2,1)}, f32[2,256,256]{2,1,0:T(8,128)}, f32[2,256,256]{2,1,0:T(8,128)}) custom-call(s32[12]{0:T(128)} %bitcast.10, bf16[12,16,16,256]{3,2,1,0:T(8,128)(2,1)} %bitcast.7, f32[2,256,256]{2,1,0:T(8,128)} %bitcast.8, f32[2,256,256]{2,1,0:T(8,128)} %bitcast.9), custom_call_target="tpu_custom_call" | custom-call | tf_op jit(solution)/shard_map/pallas_call | solution.py:359
  67.4 3.7 %shard_map.68 = (bf16[12,4,4,16,256]{4,3,2,1,0:T(8,128)(2,1)}, f32[2,256,256]{2,1,0:T(8,128)}, f32[2,256,256]{2,1,0:T(8,128)}) custom-call(s32[12]{0:T(128)} %bitcast.11, bf16[12,4,4,16,256]{4,3,2,1,0:T(8,128)(2,1)} %get-tuple-element.9.upd_ref, f32[2,256,256]{2,1,0:T(8,128)} %get-tuple-element.10.ln_ref, f32[2,256,256]{2,1,0:T(8,128)} %get-tuple-element.11.rn_ref), custom_call_target="tpu_custom_call" | custom-call | tf_op jit(solution)/shard_map/pallas_call | solution.py:390

commit v8 on v7

--- a/solution.py
+++ b/solution.py
@@ -138,7 +138,7 @@
 
     def part_copy(half, k):
         return direct(
-            0, half, k, staged.at[pl.ds(half * HALF, HALF), peer(k)], parts[half].at[k]
+            0, half, k, staged.at[half, peer(k)], parts[half].at[k]
         )
 
     def slot_copy(half, k):
@@ -151,20 +151,19 @@
         at = (half, step, axis, k)
         held = lines[half].at[axis]
         if step == 0:
-            src = dst = held.at[:, (col, row)[axis]]
+            src = dst = held.at[(col, row)[axis]]
             to = along(axis, k)
         else:
             src, dst, to = held, line_place(half, axis), along(1 - axis, k)
         return remote(src, dst, send_line.at[at], recv_line.at[at], to)
 
     def line_place(half, axis):
-        ref = upd_ref.at[pl.ds(half * HALF + axis * chunk, chunk)]
-        return ref.at[:, row] if axis == 0 else ref.at[:, :, col]
+        return upd_ref.at[half, axis, (row, col)[axis]]
 
     loads[0].wait()
     for half in range(2):
-        for p in range(half * HALF, (half + 1) * HALF):
-            staged[p] = given[block_at[p]]
+        for p in range(HALF):
+            staged[half, :, p] = given[block_at[half * HALF + p]]
         if half == 0:
             pl.semaphore_wait(barrier, n - 1)
 
@@ -189,7 +188,7 @@
         return chosen(tests, [1] * blocks) > 0
 
     def to_owners(half):
-        acc[half][...] = staged[pl.ds(half * HALF, HALF), me].astype(F32)
+        acc[half][...] = staged[half, me].astype(F32)
 
         @pl.loop(1, n)
         def _(k):
@@ -256,7 +255,7 @@
         for axis in range(2):
             for p in range(chunk):
                 value = home[half][owner_at[half * HALF + axis * chunk + p]]
-                lines[half][axis, p, (col, row)[axis]] = value
+                lines[half][axis, (col, row)[axis], p] = value
         for i in range(side - 1):
             for axis in range(2):
                 line_copy(half, 0, axis, line_turn(axis, i)).start()
@@ -321,20 +320,38 @@
 
 
 def order_kernel(
-    own_ref, upd_ref, ln_ref, rn_ref, out_ref, lo_ref, ro_ref, upd, left, right, into, out
+    own_ref, upd_ref, ln_ref, rn_ref, out_ref, lo_ref, ro_ref, upd, left, right, whole, into, out
 ):
     blocks = own_ref.shape[0]
-    _, places = ranks_of([own_ref[b] for b in range(blocks)])
-    moves = [
-        (upd_ref.at[places[b]], upd.at[b], out_ref.at[b]) for b in range(blocks)
-    ] + [(ln_ref, left, lo_ref), (rn_ref, right, ro_ref)]
-    reads = [pltpu.make_async_copy(m[0], m[1], into.at[i]) for i, m in enumerate(moves)]
-    writes = [pltpu.make_async_copy(m[1], m[2], out.at[i]) for i, m in enumerate(moves)]
+    side, chunk = upd.shape[2], upd.shape[4]
+    reads = [
+        pltpu.make_async_copy(upd_ref.at[half, axis], upd.at[half, axis], into.at[2 * half + axis])
+        for half in range(2)
+        for axis in range(2)
+    ]
+    reads += [
+        pltpu.make_async_copy(ln_ref, left, into.at[4]),
+        pltpu.make_async_copy(rn_ref, right, into.at[5]),
+    ]
     for read in reads:
         read.start()
-    for read, write in zip(reads, writes):
-        read.wait()
-        write.start()
+    _, places = ranks_of([own_ref[b] for b in range(blocks)])
+    writes = []
+    for p in range(blocks):
+        half, axis, i = p // HALF, p % HALF // chunk, p % chunk
+        if i == 0:
+            reads[2 * half + axis].wait()
+        for row in range(side):
+            for col in range(side):
+                line, at = (row, col) if axis == 0 else (col, row)
+                whole[p, row * side + col] = upd[half, axis, line, at, i]
+        block = chosen([place == p for place in places], range(blocks))
+        writes.append(pltpu.make_async_copy(whole.at[p], out_ref.at[block], out.at[p]))
+        writes[-1].start()
+    for i, ref, to in ((0, left, lo_ref), (1, right, ro_ref)):
+        reads[4 + i].wait()
+        writes.append(pltpu.make_async_copy(ref, to, out.at[blocks + i]))
+        writes[-1].start()
     for write in writes:
         write.wait()
 
@@ -349,8 +366,9 @@
     anywhere = pl.BlockSpec(memory_space=pl.ANY)
     scalars = pl.BlockSpec(memory_space=pltpu.SMEM)
     piece = (n, ROWS, width)
+    gathered = (2, 2, side, side, HALF // 2, ROWS, width)
     shapes = (
-        jax.ShapeDtypeStruct((blocks, side, side, ROWS, width), BF16),
+        jax.ShapeDtypeStruct(gathered, BF16),
         jax.ShapeDtypeStruct(pair, F32),
         jax.ShapeDtypeStruct(pair, F32),
     )
@@ -361,13 +379,13 @@
         out_shape=shapes,
         in_specs=[scalars] + [anywhere] * 3,
         out_specs=(anywhere,) * 3,
-        scratch_shapes=[vmem(tiles, BF16)] * 2
+        scratch_shapes=[vmem(tiles, BF16), vmem((2, n) + some, BF16)]
         + [vmem((n,) + some, BF16)] * 2
         + [vmem(some, F32)] * 2
         + [vmem(piece, F32)] * 4
         + [vmem(pair, F32)] * 4
         + [vmem(piece, BF16)] * 4
-        + [vmem((2, HALF // 2, side, ROWS, width), BF16)] * 2
+        + [vmem((2, side, HALF // 2, ROWS, width), BF16)] * 2
         + [
             pltpu.SMEM((blocks,), jnp.int32),
             pltpu.SMEM((blocks,), jnp.int32),
@@ -389,15 +407,16 @@
     )
     update, left_new, right_new = pl.pallas_call(
         order_kernel,
-        out_shape=shapes,
+        out_shape=(jax.ShapeDtypeStruct(tiles, BF16),) + shapes[1:],
         in_specs=[scalars] + [anywhere] * 3,
         out_specs=(anywhere,) * 3,
         scratch_shapes=[
-            vmem((blocks, side, side, ROWS, width), BF16),
+            vmem(gathered, BF16),
             vmem(pair, F32),
             vmem(pair, F32),
-            pltpu.SemaphoreType.DMA((blocks + 2,)),
-            pltpu.SemaphoreType.DMA((blocks + 2,)),
+            vmem(tiles, BF16),
+            dma((6,)),
+            dma((blocks + 2,)),
         ],
         compiler_params=pltpu.CompilerParams(vmem_limit_bytes=VMEM_BYTES),
     )(owners, update, left_new, right_new)

time: 71.5 us -> 71.1 us (level)
  no operation moved by 1% of the time
where the time goes in v8:
time: 71.1 us; the launch traced here: 70.8 us
  Pallas kernels  70.2 us (99%)
    pallas_call x1, Pallas kernels, local(): pl.pallas_call(functools.partial(kernel, side), out_shape=shapes, in_spec...  66.8 us
    pallas_call x1, Pallas kernels, local(): pl.pallas_call(order_kernel, out_shape=(jax.ShapeDtypeStruct(tiles, BF16)...  3.33 us

profile of v8, /device:TPU:480, one launch (start us, length us, event | category | flops | bytes accessed | tf_op | source)
XLA Modules:
  0.0 70.8 jit_solution(16143472486510964589)
XLA Ops:
  0.6 66.8 %shard_map.67 = (bf16[2,2,4,4,3,16,256]{6,5,4,3,2,1,0:T(8,128)(2,1)}, f32[2,256,256]{2,1,0:T(8,128)}, f32[2,256,256]{2,1,0:T(8,128)}) custom-call(s32[12]{0:T(128)} %bitcast.10, bf16[12,16,16,256]{3,2,1,0:T(8,128)(2,1)} %bitcast.7, f32[2,256,256]{2,1,0:T(8,128)} %bitcast.8, f32[2,256,256]{2,1,0:T(8,128)} %bitcast.9), custom_call_target="tpu_custom_call" | custom-call | tf_op jit(solution)/shard_map/pallas_call | solution.py:377
  67.5 3.3 %shard_map.68 = (bf16[12,16,16,256]{3,2,1,0:T(8,128)(2,1)}, f32[2,256,256]{2,1,0:T(8,128)}, f32[2,256,256]{2,1,0:T(8,128)}) custom-call(s32[12]{0:T(128)} %bitcast.11, bf16[2,2,4,4,3,16,256]{6,5,4,3,2,1,0:T(8,128)(2,1)} %get-tuple-element.9.upd_ref, f32[2,256,256]{2,1,0:T(8,128)} %get-tuple-element.10.ln_ref, f32[2,256,256]{2,1,0:T(8,128)} %get-tuple-element.11.rn_ref), custom_call_target="tpu_custom_call" | custom-call | tf_op jit(solution)/shard_map/pallas_call | solution.py:408

commit v9 on v8

--- a/solution.py
+++ b/solution.py
@@ -77,7 +77,7 @@
 
 def kernel(
     side, own_ref, g_ref, ls_ref, rs_ref, upd_ref, ln_ref, rn_ref,
-    given, staged, parts0, parts1, acc0, acc1, picked0, picked1, grad0, grad1,
+    parts, acc, picked0, picked1, grad0, grad1,
     left, right, left_out, right_out, ready0, ready1, home0, home1, lines0, lines1,
     block_at, owner_at, index_at,
     send, recv, send_line, recv_line, local,
@@ -88,7 +88,7 @@
     me = lax.axis_index("dp")
     row, col = me // side, me % side
     chunk = HALF // 2
-    parts, acc, picked, grad = (parts0, parts1), (acc0, acc1), (picked0, picked1), (grad0, grad1)
+    picked, grad = (picked0, picked1), (grad0, grad1)
     ready, home, lines = (ready0, ready1), (home0, home1), (lines0, lines1)
 
     def peer(k):
@@ -105,7 +105,7 @@
         return 1 + (i + me + core * (n // 2 - 1)) % (n - 1)
 
     loads = [
-        pltpu.make_async_copy(g_ref, given, local.at[0]),
+        pltpu.make_async_copy(g_ref.at[:, me], parts.at[0], local.at[0]),
         pltpu.make_async_copy(ls_ref, left, local.at[1]),
         pltpu.make_async_copy(rs_ref, right, local.at[2]),
     ]
@@ -117,15 +117,6 @@
     def _(k):
         pl.semaphore_signal(barrier, inc=1, device_id={"dp": peer(k)}, device_id_type=MESH)
 
-    owners = [own_ref[b] for b in range(blocks)]
-    ranks, places = ranks_of(owners)
-
-    @pl.loop(0, blocks)
-    def _(p):
-        tests = [at == p for at in places]
-        block_at[p] = chosen(tests, range(blocks))
-        owner_at[p] = chosen(tests, owners)
-
     def remote(src, dst, sent, landed, to):
         return pltpu.make_async_remote_copy(
             src_ref=src, dst_ref=dst, send_sem=sent, recv_sem=landed,
@@ -136,10 +127,8 @@
         at = (2 * what + half, k)
         return remote(src, dst, send.at[at], recv.at[at], peer(k))
 
-    def part_copy(half, k):
-        return direct(
-            0, half, k, staged.at[half, peer(k)], parts[half].at[k]
-        )
+    def part_copy(k):
+        return direct(0, 0, k, g_ref.at[:, peer(k)], parts.at[k])
 
     def slot_copy(half, k):
         return direct(1, half, k, picked[half].at[k], grad[half].at[me])
@@ -160,24 +149,28 @@
     def line_place(half, axis):
         return upd_ref.at[half, axis, (row, col)[axis]]
 
-    loads[0].wait()
-    for half in range(2):
-        for p in range(HALF):
-            staged[half, :, p] = given[block_at[half * HALF + p]]
-        if half == 0:
-            pl.semaphore_wait(barrier, n - 1)
-
-        @pl.loop(0, n - 1)
-        def _(i):
-            part_copy(half, turned_round(i)).start()
+    pl.semaphore_wait(barrier, n - 1)
+
+    @pl.loop(0, n - 1)
+    def _(i):
+        part_copy(turned_round(i)).start()
+
+    owners = [own_ref[b] for b in range(blocks)]
+    ranks, places = ranks_of(owners)
+
+    @pl.loop(0, blocks)
+    def _(p):
+        tests = [at == p for at in places]
+        block_at[p] = chosen(tests, range(blocks))
+        owner_at[p] = chosen(tests, owners)
 
     @pl.loop(0, n)
     def _(k):
         to = peer(k)
         for half in range(2):
             index = jnp.int32(0)
-            for i in range(1, HALF):
-                index = jnp.where(owner_at[half * HALF + i] == to, i, index)
+            for p in range(half * HALF, (half + 1) * HALF):
+                index = jnp.where(owner_at[p] == to, block_at[p], index)
             index_at[half, k] = index
 
     def mine(half, slot):
@@ -187,21 +180,22 @@
             tests.append((owner == me) & inside & ((rank == 0) if slot == 0 else (rank > 0)))
         return chosen(tests, [1] * blocks) > 0
 
-    def to_owners(half):
-        acc[half][...] = staged[half, me].astype(F32)
-
-        @pl.loop(1, n)
-        def _(k):
-            part_copy(half, k).wait_recv()
-            acc[half][...] += parts[half][k].astype(F32)
-
+    loads[0].wait()
+    acc[...] = parts[0].astype(F32)
+
+    @pl.loop(1, n)
+    def _(k):
+        part_copy(k).wait_recv()
+        acc[...] += parts[k].astype(F32)
+
+    for half in range(2):
         @pl.loop(0, n - 1)
         def _(i):
             k = turned_round(i)
-            picked[half][k] = acc[half][index_at[half, k]]
+            picked[half][k] = acc[index_at[half, k]]
             slot_copy(half, k).start()
 
-        grad[half][me] = acc[half][index_at[half, 0]]
+        grad[half][me] = acc[index_at[half, 0]]
 
     eye = lax.broadcasted_iota(jnp.int32, (width, width), 0) == lax.broadcasted_iota(
         jnp.int32, (width, width), 1
@@ -279,19 +273,14 @@
             rest.start()
             rests.append(rest)
 
-    to_owners(0)
     loads[1].wait()
     loads[2].wait()
-
-    def beside_first(step):
-        if step == 2:
-            to_owners(1)
 
     def beside_second(step):
         if step == 3:
             along_first(0)
 
-    solve(0, mine(0, 0), left[0], right[0], beside_first)
+    solve(0, mine(0, 0), left[0], right[0], lambda step: None)
     slot = jnp.where(mine(1, 1), 1, 0)
     used = mine(1, 0) | mine(1, 1)
     solve(1, used, left[slot], right[slot], beside_second)
@@ -305,8 +294,8 @@
 
     @pl.loop(1, n)
     def _(k):
+        part_copy(k).wait_send()
         for half in range(2):
-            part_copy(half, k).wait_send()
             slot_copy(half, k).wait_send()
             home_copy(half, k).wait_send()
 
@@ -372,16 +361,13 @@
         jax.ShapeDtypeStruct(pair, F32),
         jax.ShapeDtypeStruct(pair, F32),
     )
-    some = (HALF, ROWS, width)
     dma = pltpu.SemaphoreType.DMA
     update, left_new, right_new = pl.pallas_call(
         functools.partial(kernel, side),
         out_shape=shapes,
         in_specs=[scalars] + [anywhere] * 3,
         out_specs=(anywhere,) * 3,
-        scratch_shapes=[vmem(tiles, BF16), vmem((2, n) + some, BF16)]
-        + [vmem((n,) + some, BF16)] * 2
-        + [vmem(some, F32)] * 2
+        scratch_shapes=[vmem((n, blocks, ROWS, width), BF16), vmem((blocks, ROWS, width), F32)]
         + [vmem(piece, F32)] * 4
         + [vmem(pair, F32)] * 4
         + [vmem(piece, BF16)] * 4

time: 71.1 us -> 69.8 us (0.982)
  Pallas kernels: 70.2 us -> 68.8 us
    pallas_call x1, Pallas kernels: 66.8 us -> 65.4 us  [local(): pl.pallas_call(functools.partial(kernel, side), out_shape=shapes, in_spec...]
where the time goes in v9:
time: 69.8 us; the launch traced here: 69.4 us
  Pallas kernels  68.8 us (99%)
    pallas_call x1, Pallas kernels, local(): pl.pallas_call(functools.partial(kernel, side), out_shape=shapes, in_spec...  65.4 us
    pallas_call x1, Pallas kernels, local(): pl.pallas_call(order_kernel, out_shape=(jax.ShapeDtypeStruct(tiles, BF16)...  3.33 us

profile of v9, /device:TPU:480, one launch (start us, length us, event | category | flops | bytes accessed | tf_op | source)
XLA Modules:
  0.0 69.4 jit_solution(2543732895423988539)
XLA Ops:
  0.6 65.4 %shard_map.67 = (bf16[2,2,4,4,3,16,256]{6,5,4,3,2,1,0:T(8,128)(2,1)}, f32[2,256,256]{2,1,0:T(8,128)}, f32[2,256,256]{2,1,0:T(8,128)}) custom-call(s32[12]{0:T(128)} %bitcast.10, bf16[12,16,16,256]{3,2,1,0:T(8,128)(2,1)} %bitcast.7, f32[2,256,256]{2,1,0:T(8,128)} %bitcast.8, f32[2,256,256]{2,1,0:T(8,128)} %bitcast.9), custom_call_target="tpu_custom_call" | custom-call | tf_op jit(solution)/shard_map/pallas_call | solution.py:365
  66.1 3.3 %shard_map.68 = (bf16[12,16,16,256]{3,2,1,0:T(8,128)(2,1)}, f32[2,256,256]{2,1,0:T(8,128)}, f32[2,256,256]{2,1,0:T(8,128)}) custom-call(s32[12]{0:T(128)} %bitcast.11, bf16[2,2,4,4,3,16,256]{6,5,4,3,2,1,0:T(8,128)(2,1)} %get-tuple-element.9.upd_ref, f32[2,256,256]{2,1,0:T(8,128)} %get-tuple-element.10.ln_ref, f32[2,256,256]{2,1,0:T(8,128)} %get-tuple-element.11.rn_ref), custom_call_target="tpu_custom_call" | custom-call | tf_op jit(solution)/shard_map/pallas_call | solution.py:394

commit v10 on v9

--- a/solution.py
+++ b/solution.py
@@ -67,12 +67,6 @@
 
     def next_factor(self):
         self.factor = split(jnp.where(self.eye, 1.25, 0.0) - 0.25 * self.power)
-
-    def advance(self):
-        square = split(product(self.factor, self.factor))
-        fourth = split(product(square, square))
-        self.power = product(fourth, split(self.power))
-        self.next_factor()
 
 
 def kernel(
@@ -221,19 +215,29 @@
                 ):
                     rest = out[0] if slot == 0 else DECAY * old[1]
                     out[slot] = jnp.where(here, new, rest)
-        first, second = Root(left_new, eye), Root(right_new, eye)
-        moved = product(split(product(first.factor, plain)), second.factor)
+        count = 1.0 / (width * width)
+        size = jnp.sqrt(total(value * value) * count)
+        first, second = roots = Root(left_new, eye), Root(right_new, eye)
+        moved = plain
         for step in range(1, ITERS):
-            first.advance()
-            second.advance()
+            squares = [product(root.factor, root.factor) for root in roots]
+            half_way = product(first.factor, moved)
+            squares = [split(square) for square in squares]
+            half_way = split(half_way)
+            fourths = [product(square, square) for square in squares]
+            moved = product(half_way, second.factor)
+            fourths = [split(fourth) for fourth in fourths]
+            powers = [split(root.power) for root in roots]
+            moved = split(moved)
+            for root, fourth, power in zip(roots, fourths, powers):
+                root.power = product(fourth, power)
+            for root in roots:
+                root.next_factor()
             beside(step)
-            moved = product(split(product(first.factor, split(moved))), second.factor)
-        direction = (first.gain * second.gain) * moved
-        count = 1.0 / (width * width)
-        ratio = jnp.sqrt(total(value * value) * count) / jnp.sqrt(
-            total(direction * direction) * count + 1e-06
-        )
-        ready[half][...] = (direction * ratio).astype(BF16).reshape(ready[half].shape)
+        moved = product(split(product(first.factor, moved)), second.factor)
+        gain = first.gain * second.gain
+        ratio = size / jnp.sqrt(gain * gain * total(moved * moved) * count + 1e-06)
+        ready[half][...] = (moved * (gain * ratio)).astype(BF16).reshape(ready[half].shape)
 
         @pl.loop(0, n - 1)
         def _(i):

time: 69.8 us -> 69.8 us (level)
  the two profiles are of different devices: /device:TPU:480 before, /device:TPU:2 now
where the time goes in v10:
time: 69.8 us; the launch traced here: 69.7 us
  Pallas kernels  69 us (99%)
    pallas_call x1, Pallas kernels, local(): pl.pallas_call(functools.partial(kernel, side), out_shape=shapes, in_spec...  65.7 us
    pallas_call x1, Pallas kernels, local(): pl.pallas_call(order_kernel, out_shape=(jax.ShapeDtypeStruct(tiles, BF16)...  3.33 us

profile of v10, /device:TPU:2, one launch (start us, length us, event | category | flops | bytes accessed | tf_op | source)
XLA Modules:
  0.0 69.7 jit_solution(16481629065396388450)
XLA Ops:
  0.6 65.7 %shard_map.67 = (bf16[2,2,4,4,3,16,256]{6,5,4,3,2,1,0:T(8,128)(2,1)}, f32[2,256,256]{2,1,0:T(8,128)}, f32[2,256,256]{2,1,0:T(8,128)}) custom-call(s32[12]{0:T(128)} %bitcast.10, bf16[12,16,16,256]{3,2,1,0:T(8,128)(2,1)} %bitcast.7, f32[2,256,256]{2,1,0:T(8,128)} %bitcast.8, f32[2,256,256]{2,1,0:T(8,128)} %bitcast.9), custom_call_target="tpu_custom_call" | custom-call | tf_op jit(solution)/shard_map/pallas_call | solution.py:369
  66.3 3.3 %shard_map.68 = (bf16[12,16,16,256]{3,2,1,0:T(8,128)(2,1)}, f32[2,256,256]{2,1,0:T(8,128)}, f32[2,256,256]{2,1,0:T(8,128)}) custom-call(s32[12]{0:T(128)} %bitcast.11, bf16[2,2,4,4,3,16,256]{6,5,4,3,2,1,0:T(8,128)(2,1)} %get-tuple-element.9.upd_ref, f32[2,256,256]{2,1,0:T(8,128)} %get-tuple-element.10.ln_ref, f32[2,256,256]{2,1,0:T(8,128)} %get-tuple-element.11.rn_ref), custom_call_target="tpu_custom_call" | custom-call | tf_op jit(solution)/shard_map/pallas_call | solution.py:398

commit v11 on v10

--- a/solution.py
+++ b/solution.py
@@ -71,9 +71,9 @@
 
 def kernel(
     side, own_ref, g_ref, ls_ref, rs_ref, upd_ref, ln_ref, rn_ref,
-    parts, acc, picked0, picked1, grad0, grad1,
+    parts, sums, second_sums, acc, picked0, picked1, grad0, grad1,
     left, right, left_out, right_out, ready0, ready1, home0, home1, lines0, lines1,
-    block_at, owner_at, index_at,
+    block_at, owner_at, index_at, send_sum, recv_sum,
     send, recv, send_line, recv_line, local,
 ):
     n = side * side
@@ -99,10 +99,18 @@
         return 1 + (i + me + core * (n // 2 - 1)) % (n - 1)
 
     loads = [
-        pltpu.make_async_copy(g_ref.at[:, me], parts.at[0], local.at[0]),
         pltpu.make_async_copy(ls_ref, left, local.at[1]),
         pltpu.make_async_copy(rs_ref, right, local.at[2]),
     ]
+    pieces = [(j, kind) for j in range(2) for kind in range(2)]
+    for j, kind in pieces:
+        loads.append(
+            pltpu.make_async_copy(
+                g_ref.at[pl.ds(kind * HALF + j * chunk, chunk), (col, row)[kind]],
+                parts.at[kind, j, 0],
+                local.at[9 + 2 * j + kind],
+            )
+        )
     for load in loads:
         load.start()
     barrier = pltpu.get_barrier_semaphore()
@@ -121,8 +129,19 @@
         at = (2 * what + half, k)
         return remote(src, dst, send.at[at], recv.at[at], peer(k))
 
-    def part_copy(k):
-        return direct(0, 0, k, g_ref.at[:, peer(k)], parts.at[k])
+    def part_copy(j, kind, k):
+        src = g_ref.at[pl.ds(kind * HALF + j * chunk, chunk), ((col, row)[kind] + k) % side]
+        at = (0, kind, j, k)
+        return remote(
+            src, parts.at[kind, j, k], send_sum.at[at], recv_sum.at[at], along(kind, k)
+        )
+
+    def sum_copy(j, kind, k):
+        src = sums.at[kind, j, ((row, col)[kind] + k) % side]
+        at = (1, kind, j, k)
+        return remote(
+            src, second_sums.at[kind, j, k], send_sum.at[at], recv_sum.at[at], along(1 - kind, k)
+        )
 
     def slot_copy(half, k):
         return direct(1, half, k, picked[half].at[k], grad[half].at[me])
@@ -145,9 +164,10 @@
 
     pl.semaphore_wait(barrier, n - 1)
 
-    @pl.loop(0, n - 1)
-    def _(i):
-        part_copy(turned_round(i)).start()
+    for j in range(2):
+        for i in range(1, side):
+            for kind in range(2):
+                part_copy(j, kind, i).start()
 
     owners = [own_ref[b] for b in range(blocks)]
     ranks, places = ranks_of(owners)
@@ -174,13 +194,23 @@
             tests.append((owner == me) & inside & ((rank == 0) if slot == 0 else (rank > 0)))
         return chosen(tests, [1] * blocks) > 0
 
-    loads[0].wait()
-    acc[...] = parts[0].astype(F32)
-
-    @pl.loop(1, n)
-    def _(k):
-        part_copy(k).wait_recv()
-        acc[...] += parts[k].astype(F32)
+    for number, (j, kind) in enumerate(pieces):
+        loads[2 + number].wait()
+        for k in range(1, side):
+            part_copy(j, kind, k).wait_recv()
+
+        @pl.loop(0, side)
+        def _(v):
+            sums[kind, j, v] = sum(parts[kind, j, k, :, v].astype(F32) for k in range(side))
+
+        for k in range(1, side):
+            sum_copy(j, kind, k).start()
+    for j, kind in pieces:
+        for k in range(1, side):
+            sum_copy(j, kind, k).wait_recv()
+        acc[pl.ds(kind * HALF + j * chunk, chunk)] = sums[kind, j, (row, col)[kind]] + (
+            second_sums[kind, j, 1] + second_sums[kind, j, 2] + second_sums[kind, j, 3]
+        )
 
     for half in range(2):
         @pl.loop(0, n - 1)
@@ -191,6 +221,12 @@
 
         grad[half][me] = acc[index_at[half, 0]]
 
+    def low_mine(half):
+        tests = []
+        for owner, at in zip(owners[:HALF], places[:HALF]):
+            tests.append((owner == me) & ((at < HALF) if half == 0 else (at >= HALF)))
+        return chosen(tests, [1] * HALF) > 0
+
     eye = lax.broadcasted_iota(jnp.int32, (width, width), 0) == lax.broadcasted_iota(
         jnp.int32, (width, width), 1
     )
@@ -200,7 +236,9 @@
         def _(k):
             slot_copy(half, k).wait_recv()
 
-        value = jnp.where(used, grad[half][...].reshape(width, width), 0.0)
+        across = jnp.stack([grad[half][(i % side) * side + i // side] for i in range(n)])
+        value = jnp.where(low_mine(half), across, grad[half][...]).reshape(width, width)
+        value = jnp.where(used, value, 0.0)
         plain, turned = split(value), split(value.T)
         left_new = DECAY * left_old + (1.0 - DECAY) * product(plain, turned)
         right_new = DECAY * right_old + (1.0 - DECAY) * product(turned, plain)
@@ -277,8 +315,8 @@
             rest.start()
             rests.append(rest)
 
+    loads[0].wait()
     loads[1].wait()
-    loads[2].wait()
 
     def beside_second(step):
         if step == 3:
@@ -298,11 +336,14 @@
 
     @pl.loop(1, n)
     def _(k):
-        part_copy(k).wait_send()
         for half in range(2):
             slot_copy(half, k).wait_send()
             home_copy(half, k).wait_send()
 
+    for j, kind in pieces:
+        for k in range(1, side):
+            part_copy(j, kind, k).wait_send()
+            sum_copy(j, kind, k).wait_send()
     for half in range(2):
         for axis in range(2):
             for k in range(1, side):
@@ -371,7 +412,12 @@
         out_shape=shapes,
         in_specs=[scalars] + [anywhere] * 3,
         out_specs=(anywhere,) * 3,
-        scratch_shapes=[vmem((n, blocks, ROWS, width), BF16), vmem((blocks, ROWS, width), F32)]
+        scratch_shapes=[
+            vmem((2, 2, side, HALF // 2, side, ROWS, width), BF16),
+            vmem((2, 2, side, HALF // 2, ROWS, width), F32),
+            vmem((2, 2, side, HALF // 2, ROWS, width), F32),
+            vmem((blocks, ROWS, width), F32),
+        ]
         + [vmem(piece, F32)] * 4
         + [vmem(pair, F32)] * 4
         + [vmem(piece, BF16)] * 4
@@ -380,18 +426,20 @@
             pltpu.SMEM((blocks,), jnp.int32),
             pltpu.SMEM((blocks,), jnp.int32),
             pltpu.SMEM((2, n), jnp.int32),
+            dma((2, 2, 2, side)),
+            dma((2, 2, 2, side)),
             dma((6, n)),
             dma((6, n)),
             dma((2, 2, 2, side)),
             dma((2, 2, 2, side)),
-            dma((9,)),
+            dma((13,)),
         ],
         compiler_params=pltpu.CompilerParams(
             collective_id=0, has_side_effects=True, vmem_limit_bytes=VMEM_BYTES
         ),
     )(
         owners,
-        grad_parts.reshape(tiles),
+        grad_parts.reshape(blocks, side, side, ROWS, width),
         left_stats.reshape(pair),
         right_stats.reshape(pair),
     )

time: 69.8 us -> 65.9 us (0.944)
  the two profiles are of different devices: /device:TPU:2 before, /device:TPU:480 now
where the time goes in v11:
time: 65.9 us; the launch traced here: 65.4 us
  Pallas kernels  64.8 us (98%)
    pallas_call x1, Pallas kernels, local(): pl.pallas_call(functools.partial(kernel, side), out_shape=shapes, in_spec...  61.4 us
    pallas_call x1, Pallas kernels, local(): pl.pallas_call(order_kernel, out_shape=(jax.ShapeDtypeStruct(tiles, BF16)...  3.33 us

profile of v11, /device:TPU:480, one launch (start us, length us, event | category | flops | bytes accessed | tf_op | source)
XLA Modules:
  0.0 65.4 jit_solution(1373315974524488575)
XLA Ops:
  0.6 61.4 %shard_map.67 = (bf16[2,2,4,4,3,16,256]{6,5,4,3,2,1,0:T(8,128)(2,1)}, f32[2,256,256]{2,1,0:T(8,128)}, f32[2,256,256]{2,1,0:T(8,128)}) custom-call(s32[12]{0:T(128)} %bitcast.10, bf16[12,4,4,16,256]{4,3,2,1,0:T(8,128)(2,1)} %bitcast.7, f32[2,256,256]{2,1,0:T(8,128)} %bitcast.8, f32[2,256,256]{2,1,0:T(8,128)} %bitcast.9), custom_call_target="tpu_custom_call" | custom-call | tf_op jit(solution)/shard_map/pallas_call | solution.py:410
  62.1 3.3 %shard_map.68 = (bf16[12,16,16,256]{3,2,1,0:T(8,128)(2,1)}, f32[2,256,256]{2,1,0:T(8,128)}, f32[2,256,256]{2,1,0:T(8,128)}) custom-call(s32[12]{0:T(128)} %bitcast.11, bf16[2,2,4,4,3,16,256]{6,5,4,3,2,1,0:T(8,128)(2,1)} %get-tuple-element.9.upd_ref, f32[2,256,256]{2,1,0:T(8,128)} %get-tuple-element.10.ln_ref, f32[2,256,256]{2,1,0:T(8,128)} %get-tuple-element.11.rn_ref), custom_call_target="tpu_custom_call" | custom-call | tf_op jit(solution)/shard_map/pallas_call | solution.py:446

commit v12 on v11

--- a/solution.py
+++ b/solution.py
@@ -12,6 +12,7 @@
 RIDGE = 0.01
 ROWS = 16
 VMEM_BYTES = 56 * 1024 * 1024
+FAR_FIRST = (2, 1, 3)
 HALF = 6
 BF16, F32 = jnp.bfloat16, jnp.float32
 MESH = pl.DeviceIdType.MESH
@@ -165,7 +166,7 @@
     pl.semaphore_wait(barrier, n - 1)
 
     for j in range(2):
-        for i in range(1, side):
+        for i in FAR_FIRST:
             for kind in range(2):
                 part_copy(j, kind, i).start()
 
@@ -203,7 +204,7 @@
         def _(v):
             sums[kind, j, v] = sum(parts[kind, j, k, :, v].astype(F32) for k in range(side))
 
-        for k in range(1, side):
+        for k in FAR_FIRST:
             sum_copy(j, kind, k).start()
     for j, kind in pieces:
         for k in range(1, side):
@@ -292,22 +293,19 @@
             for p in range(chunk):
                 value = home[half][owner_at[half * HALF + axis * chunk + p]]
                 lines[half][axis, (col, row)[axis], p] = value
-        for i in range(side - 1):
+        for k in FAR_FIRST:
             for axis in range(2):
-                line_copy(half, 0, axis, line_turn(axis, i)).start()
+                line_copy(half, 0, axis, k).start()
 
     rests = []
-
-    def line_turn(axis, i):
-        return 1 + (i + row + col + core + axis) % (side - 1)
 
     def along_second(half):
         for axis in range(2):
             for k in range(1, side):
                 line_copy(half, 0, axis, k).wait_recv()
-        for i in range(side - 1):
+        for k in FAR_FIRST:
             for axis in range(2):
-                line_copy(half, 1, axis, line_turn(axis, i)).start()
+                line_copy(half, 1, axis, k).start()
         for axis in range(2):
             rest = pltpu.make_async_copy(
                 lines[half].at[axis], line_place(half, axis), local.at[5 + 2 * half + axis]

time: 65.9 us -> 64.7 us (0.982)
  Pallas kernels: 64.8 us -> 63.9 us
    pallas_call x1, Pallas kernels: 61.4 us -> 60.6 us  [local(): pl.pallas_call(functools.partial(kernel, side), out_shape=shapes, in_spec...]
where the time goes in v12:
time: 64.7 us; the launch traced here: 64.5 us
  Pallas kernels  63.9 us (99%)
    pallas_call x1, Pallas kernels, local(): pl.pallas_call(functools.partial(kernel, side), out_shape=shapes, in_spec...  60.6 us
    pallas_call x1, Pallas kernels, local(): pl.pallas_call(order_kernel, out_shape=(jax.ShapeDtypeStruct(tiles, BF16)...  3.33 us

profile of v12, /device:TPU:480, one launch (start us, length us, event | category | flops | bytes accessed | tf_op | source)
XLA Modules:
  0.0 64.5 jit_solution(16359781115236240923)
XLA Ops:
  0.6 60.6 %shard_map.67 = (bf16[2,2,4,4,3,16,256]{6,5,4,3,2,1,0:T(8,128)(2,1)}, f32[2,256,256]{2,1,0:T(8,128)}, f32[2,256,256]{2,1,0:T(8,128)}) custom-call(s32[12]{0:T(128)} %bitcast.10, bf16[12,4,4,16,256]{4,3,2,1,0:T(8,128)(2,1)} %bitcast.7, f32[2,256,256]{2,1,0:T(8,128)} %bitcast.8, f32[2,256,256]{2,1,0:T(8,128)} %bitcast.9), custom_call_target="tpu_custom_call" | custom-call | tf_op jit(solution)/shard_map/pallas_call | solution.py:408
  61.2 3.3 %shard_map.68 = (bf16[12,16,16,256]{3,2,1,0:T(8,128)(2,1)}, f32[2,256,256]{2,1,0:T(8,128)}, f32[2,256,256]{2,1,0:T(8,128)}) custom-call(s32[12]{0:T(128)} %bitcast.11, bf16[2,2,4,4,3,16,256]{6,5,4,3,2,1,0:T(8,128)(2,1)} %get-tuple-element.9.upd_ref, f32[2,256,256]{2,1,0:T(8,128)} %get-tuple-element.10.ln_ref, f32[2,256,256]{2,1,0:T(8,128)} %get-tuple-element.11.rn_ref), custom_call_target="tpu_custom_call" | custom-call | tf_op jit(solution)/shard_map/pallas_call | solution.py:444
